TPU v7x, 32 devices: a whole 2x2x4 slice. The times are simulated.
32 devices in a mesh: blk: 8 (over y, x, core), uly: 4 (over z).
Axes of the slice: x: 2, y: 2, z: 4, core: 2. Of those that a mesh axis runs over, the one named last changes fastest.
Arguments:
- tokens: bfloat16 [1536, 2048], P(('blk', 'uly')), may hold values from -6 to 6
- mod_shift: float32 [2048], replicated, may hold values from -3 to 3
- mod_scale: float32 [2048], replicated, may hold values from -2.5 to 2.5
- mod_gate: float32 [2048], replicated, may hold values from 0.25 to 1.5
- w_query: bfloat16 [2048, 2048], P(None, 'uly'), may hold values from -0.125 to 0.125
- w_key: bfloat16 [2048, 2048], P(None, 'uly'), may hold values from -0.125 to 0.125
- w_value: bfloat16 [2048, 2048], P(None, 'uly'), may hold values from -0.125 to 0.125
- w_out: bfloat16 [2048, 2048], P('uly'), may hold values from -0.125 to 0.125
- score_gain: float32 [32], replicated, may hold values from 4 to 40, as said below
Outputs:
- block_out: bfloat16 [1536, 2048], P(('blk', 'uly'))
Inputs may be any that keep to these rules, and one draw needn't show every extreme that they name: `score_gain`: one positive factor for each head.
All inputs are finite; a program needn't handle non-finite values.
Results may differ from a plain program's by a relative error of at most 0.012.
The roundings to bfloat16 on the way count: a program that leaves them out, or rounds other values in their place, can miss the bound.
Values may be sent and summed in bfloat16 or wider, within the bound.
A program may use at most 192 MiB of HBM per device.

v0:
```python
import functools
import math

import jax
import jax.numpy as jnp
from jax import lax
from jax.experimental import pallas as pl
from jax.experimental.pallas import tpu as pltpu
from jax.sharding import PartitionSpec as P

D = 2048
HEADS = 32
LOG2E = math.log2(math.e)
MESH = pl.DeviceIdType.MESH


def kernel(
    nb, nz, tok_h, shift_h, scale_h, gate_h, gain_h, wq, wk, wv, wo, out,
    tok, shift, scale, gate, gain, mod, wq_v, wk_v, wv_v, wo_v, snd, rcv, asnd, arcv, own, rsnd, rrcv,
    wsem, gs, gr, fs, hs, hr, bs, br, rs, rr,
):
    width = D // HEADS
    rows = tok.shape[0]
    block = nz * rows
    half = block // 2
    tile = rrcv.shape[-1]
    parts = D // tile
    mb, mz = lax.axis_index("blk"), lax.axis_index("uly")

    pairs = (
        (tok_h, tok), (shift_h, shift), (scale_h, scale), (wq, wq_v), (wk, wk_v), (wv, wv_v),
        (wo, wo_v), (gate_h, gate), (gain_h, gain),
    )
    loads = [
        pltpu.make_async_copy(src, dst, wsem.at[i])
        for i, (src, dst) in enumerate(pairs)
    ]
    for load in loads:
        load.start()

    barrier = pltpu.get_barrier_semaphore()
    for j in range(1, nz):
        pl.semaphore_signal(barrier, inc=1, device_id={"uly": lax.rem(mz + j, nz)}, device_id_type=MESH)
    for j in range(1, nb):
        pl.semaphore_signal(barrier, inc=1, device_id={"blk": lax.rem(mb + j, nb)}, device_id_type=MESH)

    def order(k):
        if nz != 4:
            return lax.rem(mz + k, nz)
        high = mz // 2
        near = mz + 1 - 2 * lax.rem(mz, 2)
        return jnp.where(k == 0, mz, jnp.where(k == 1, near, jnp.where(k == 2, 2 - high, 3 - 3 * high)))

    for load in loads[:3]:
        load.wait()
    relayed = nz == 4
    direct = (2, 1) if relayed else tuple(range(nz - 1, 0, -1))
    middle = (mz + 1) // 2 == 1

    values = tok[...].astype(jnp.float32)
    center = values - jnp.mean(values, axis=-1, keepdims=True)
    spread = jnp.mean(center * center, axis=-1, keepdims=True)
    normed = center * lax.rsqrt(spread + 1e-06)
    mod[mz] = (normed * (1.0 + scale[...]) + shift[...]).astype(jnp.bfloat16)

    pl.semaphore_wait(barrier, nz - 1 + nb - 1)

    def gather(z):
        return pltpu.make_async_remote_copy(
            src_ref=mod.at[mz], dst_ref=mod.at[mz], send_sem=gs.at[z], recv_sem=gr.at[mz],
            device_id={"uly": z}, device_id_type=MESH)

    def gathered(z):
        return pltpu.make_async_remote_copy(
            src_ref=mod.at[z], dst_ref=mod.at[z], send_sem=gs.at[z], recv_sem=gr.at[z],
            device_id={"uly": z}, device_id_type=MESH)

    def forward(z):
        return pltpu.make_async_remote_copy(
            src_ref=mod.at[z], dst_ref=mod.at[z], send_sem=fs.at[z], recv_sem=gr.at[z],
            device_id={"uly": order(1)}, device_id_type=MESH)

    for k in direct:
        gather(order(k)).start()
    for load in loads[3:6]:
        load.wait()

    def spot(b, z):
        return pl.ds(pl.multiple_of((b * nz + z) * rows, rows), rows)

    def heads_to(z, b):
        return pltpu.make_async_remote_copy(
            src_ref=snd.at[z, b], dst_ref=rcv.at[:, spot(mb, z), :], send_sem=hs.at[z, b],
            recv_sem=hr.at[z, mb], device_id={"blk": b}, device_id_type=MESH)

    def heads_from(z, b):
        return pltpu.make_async_remote_copy(
            src_ref=snd.at[z, b], dst_ref=rcv.at[:, spot(b, z), :], send_sem=hs.at[z, b],
            recv_sem=hr.at[z, b], device_id={"blk": b}, device_id_type=MESH)

    def piece(k, carry):
        z = order(k)

        @pl.when(k > 0)
        def _():
            gathered(z).wait_recv()

        if relayed:

            @pl.when((k > 1) & middle)
            def _():
                forward(z).start()

        x = mod[z]
        query = jnp.dot(x, wq_v[...], preferred_element_type=jnp.float32)
        key = jnp.dot(x, wk_v[...], preferred_element_type=jnp.float32)
        value = jnp.dot(x, wv_v[...], preferred_element_type=jnp.float32)

        def unit(part):
            power = jnp.mean(part * part, axis=-1, keepdims=True)
            return part * lax.rsqrt(power + 1e-06)

        for h in range(nb):
            cols = slice(h * width, (h + 1) * width)
            snd[z, h, 0] = jnp.concatenate([unit(key[:, cols]), value[:, cols]], axis=1).astype(jnp.bfloat16)
            line = unit(query[:, cols])
            snd[z, h, 1] = jnp.concatenate([line, jnp.zeros_like(line)], axis=1).astype(jnp.bfloat16)
        rcv[:, spot(mb, z), :] = snd[z, mb]

        def send(j, carry):
            heads_to(z, lax.rem(mb + j, nb)).start()
            return carry

        lax.fori_loop(1, nb, send, 0)
        return carry

    lax.fori_loop(0, nz, piece, 0)

    def arrive(i, carry):
        heads_from(order(i // (nb - 1)), lax.rem(mb + 1 + lax.rem(i, nb - 1), nb)).wait_recv()
        return carry

    lax.fori_loop(0, nz * (nb - 1), arrive, 0)

    loads[8].wait()
    chosen = lax.broadcasted_iota(jnp.int32, gain.shape, 1) == mz * nb + mb
    factor = jnp.sum(jnp.where(chosen, gain[...], 0.0), axis=-1, keepdims=True) * (LOG2E / math.sqrt(width))

    def back_to(b):
        return pltpu.make_async_remote_copy(
            src_ref=asnd.at[b], dst_ref=arcv.at[mb], send_sem=bs.at[b], recv_sem=br.at[mb],
            device_id={"blk": b}, device_id_type=MESH)

    def back_from(b):
        return pltpu.make_async_remote_copy(
            src_ref=asnd.at[b], dst_ref=arcv.at[b], send_sem=bs.at[b], recv_sem=br.at[b],
            device_id={"blk": b}, device_id_type=MESH)

    def attend(k, carry):
        b = lax.rem(mb + k, nb)
        q = rcv[1, pl.ds(pl.multiple_of(b * block, block), block), :]
        kv = rcv[0]
        scores = lax.dot_general(q, kv, (((1,), (1,)), ((), ())), preferred_element_type=jnp.float32)
        top = jnp.max(scores, axis=-1, keepdims=True)
        expo = jnp.exp2((scores - top) * factor)
        total = jnp.sum(expo, axis=-1, keepdims=True)
        summed = jnp.dot(expo.astype(jnp.bfloat16), kv, preferred_element_type=jnp.float32) / total
        packed = jnp.concatenate([summed[:half, width:], summed[half:, width:]], axis=1)
        asnd[b] = packed.astype(jnp.bfloat16)

        @pl.when(k < nb)
        def _():
            back_to(b).start()

        return carry

    lax.fori_loop(1, nb + 1, attend, 0)
    arcv[mb] = asnd[mb]
    loads[6].wait()
    loads[7].wait()
    for j in range(1, nb):
        back_from(lax.rem(mb + j, nb)).wait_recv()

    pieces = [arcv[h] for h in range(nb)]
    attended = jnp.concatenate(
        [
            jnp.concatenate([part[:, :width] for part in pieces], axis=1),
            jnp.concatenate([part[:, width:] for part in pieces], axis=1),
        ],
        axis=0,
    )

    def sum_to(n, z):
        return pltpu.make_async_remote_copy(
            src_ref=rsnd.at[n, z], dst_ref=rrcv.at[n, mz], send_sem=rs.at[n, z], recv_sem=rr.at[n, mz],
            device_id={"uly": z}, device_id_type=MESH)

    def sum_from(n, z):
        return pltpu.make_async_remote_copy(
            src_ref=rsnd.at[n, z], dst_ref=rrcv.at[n, z], send_sem=rs.at[n, z], recv_sem=rr.at[n, z],
            device_id={"uly": z}, device_id_type=MESH)

    for n in range(parts):
        part = jnp.dot(attended, wo_v[:, n * tile : (n + 1) * tile], preferred_element_type=jnp.float32)
        for z in range(nz):
            own[n, z] = part[z * rows : (z + 1) * rows]
            rsnd[n, z] = part[z * rows : (z + 1) * rows].astype(jnp.bfloat16)
        for k in range(nz - 1, 0, -1):
            sum_to(n, order(k)).start()
    for n in range(parts):
        total = own[n, mz]
        for k in range(1, nz):
            z = order(k)
            sum_from(n, z).wait_recv()
            total = total + rrcv[n, z].astype(jnp.float32)
        cols = slice(n * tile, (n + 1) * tile)
        out[:, cols] = (tok[:, cols].astype(jnp.float32) + gate[:, cols] * total).astype(jnp.bfloat16)

    for k in direct:
        gather(order(k)).wait_send()
    if relayed:

        @pl.when(middle)
        def _():
            for k in (2, 3):
                forward(order(k)).wait_send()


    def sent(i, carry):
        heads_to(order(i // (nb - 1)), lax.rem(mb + 1 + lax.rem(i, nb - 1), nb)).wait_send()
        return carry

    lax.fori_loop(0, nz * (nb - 1), sent, 0)
    for j in range(1, nb):
        back_to(lax.rem(mb + j, nb)).wait_send()
    for n in range(parts):
        for k in range(1, nz):
            sum_to(n, order(k)).wait_send()


def fused(nb, nz, tokens, mod_shift, mod_scale, mod_gate, w_query, w_key, w_value, w_out, score_gain):
    rows = tokens.shape[0]
    cols = w_query.shape[1]
    tile = 512
    parts = D // tile
    bf16, f32 = jnp.bfloat16, jnp.float32
    vmem = pl.BlockSpec(memory_space=pltpu.VMEM)
    hbm = pl.BlockSpec(memory_space=pltpu.HBM)
    dma = pltpu.SemaphoreType.DMA
    return pl.pallas_call(
        functools.partial(kernel, nb, nz),
        out_shape=jax.ShapeDtypeStruct((rows, D), bf16),
        in_specs=[hbm] * 9,
        out_specs=vmem,
        scratch_shapes=[
            pltpu.VMEM((rows, D), bf16),
            pltpu.VMEM((1, D), f32),
            pltpu.VMEM((1, D), f32),
            pltpu.VMEM((1, D), f32),
            pltpu.VMEM((1, HEADS), f32),
            pltpu.VMEM((nz, rows, D), bf16),
            pltpu.VMEM((D, cols), bf16),
            pltpu.VMEM((D, cols), bf16),
            pltpu.VMEM((D, cols), bf16),
            pltpu.VMEM((cols, D), bf16),
            pltpu.VMEM((nz, nb, 2, rows, 128), bf16),
            pltpu.VMEM((2, nb * nz * rows, 128), bf16),
            pltpu.VMEM((nb, nz * rows // 2, 128), bf16),
            pltpu.VMEM((nb, nz * rows // 2, 128), bf16),
            pltpu.VMEM((parts, nz, rows, tile), f32),
            pltpu.VMEM((parts, nz, rows, tile), bf16),
            pltpu.VMEM((parts, nz, rows, tile), bf16),
            dma((9,)),
            dma((nz,)),
            dma((nz,)),
            dma((nz,)),
            dma((nz, nb)),
            dma((nz, nb)),
            dma((nb,)),
            dma((nb,)),
            dma((parts, nz)),
            dma((parts, nz)),
        ],
        compiler_params=pltpu.CompilerParams(
            collective_id=0, has_side_effects=True, vmem_limit_bytes=56 * 1024 * 1024
        ),
    )(
        tokens, mod_shift[None], mod_scale[None], mod_gate[None], score_gain[None],
        w_query, w_key, w_value, w_out,
    )


def modulate(tokens, mod_shift, mod_scale):
    values = tokens.astype(jnp.float32)
    center = values - jnp.mean(values, axis=-1, keepdims=True)
    spread = jnp.mean(center * center, axis=-1, keepdims=True)
    normed = center * lax.rsqrt(spread + 1e-06)
    return (normed * (1.0 + mod_scale) + mod_shift).astype(jnp.bfloat16)


def head_norm(projected, width):
    count = projected.shape[0]
    split = projected.reshape(count, -1, width)
    power = jnp.mean(split * split, axis=-1, keepdims=True)
    return (split * lax.rsqrt(power + 1e-06)).reshape(count, -1).astype(jnp.bfloat16)


def body(tokens, mod_shift, mod_scale, mod_gate, w_query, w_key, w_value, w_out, score_gain):
    width = D // HEADS
    local_cols = w_query.shape[1]
    local_heads = local_cols // width
    modded = modulate(tokens, mod_shift, mod_scale)
    piece = lax.all_gather(modded, "uly", axis=0, tiled=True)
    joined = jnp.concatenate(
        [
            jnp.dot(piece, w_query, preferred_element_type=jnp.float32),
            jnp.dot(piece, w_key, preferred_element_type=jnp.float32),
            jnp.dot(piece, w_value, preferred_element_type=jnp.float32),
        ],
        axis=1,
    )
    queries = head_norm(joined[:, :local_cols], width)
    keys = head_norm(joined[:, local_cols : 2 * local_cols], width)
    values = joined[:, 2 * local_cols :].astype(jnp.bfloat16)
    gains = lax.dynamic_slice_in_dim(score_gain, lax.axis_index("uly") * local_heads, local_heads)
    factors = gains / math.sqrt(width)
    rows = queries.shape[0]
    query_heads = queries.reshape(rows, local_heads, width)
    initial = (
        jnp.full((local_heads, rows), -jnp.inf, jnp.float32),
        jnp.zeros((local_heads, rows), jnp.float32),
        jnp.zeros((local_heads, rows, width), jnp.float32),
    )
    key_piece = lax.all_gather(keys, "blk", axis=0, tiled=True)
    value_piece = lax.all_gather(values, "blk", axis=0, tiled=True)
    count = key_piece.shape[0]
    groups = count // rows
    limit = max(rows, 1024)
    depth = max(
        [step for step in range(1, groups + 1) if groups % step == 0 and step * rows <= limit]
    )
    stride = depth * rows
    key_blocks = key_piece.reshape(count // stride, stride, local_heads, width)
    value_blocks = value_piece.reshape(count // stride, stride, local_heads, width)

    def one_block(carry, blocks):
        run_max, run_total, run_acc = carry
        key_block, value_block = blocks
        scores = jnp.einsum(
            "rhd,khd->hrk", query_heads, key_block, preferred_element_type=jnp.float32
        )
        scores = scores * factors[:, None, None]
        new_max = jnp.maximum(run_max, jnp.max(scores, axis=-1))
        expo = jnp.exp(scores - new_max[..., None])
        rescale = jnp.exp(run_max - new_max)
        new_total = run_total * rescale + jnp.sum(expo, axis=-1)
        summed = jnp.einsum(
            "hrk,khd->hrd",
            expo.astype(jnp.bfloat16),
            value_block,
            preferred_element_type=jnp.float32,
        )
        new_acc = run_acc * rescale[..., None] + summed
        return ((new_max, new_total, new_acc), None)

    result, unused = lax.scan(one_block, initial, (key_blocks, value_blocks))
    run_max, run_total, run_acc = result
    attended = (run_acc / run_total[..., None]).astype(jnp.bfloat16)
    attended = attended.transpose(1, 0, 2).reshape(rows, local_cols)
    returned = lax.all_to_all(attended, "uly", split_axis=0, concat_axis=1, tiled=True)
    projected = jnp.dot(
        returned,
        lax.all_gather(w_out, "uly", axis=0, tiled=True),
        preferred_element_type=jnp.float32,
    )
    return (tokens.astype(jnp.float32) + mod_gate * projected).astype(jnp.bfloat16)


def solution(mesh):
    in_specs = (
        P(("blk", "uly"), None),
        P(),
        P(),
        P(),
        P(None, "uly"),
        P(None, "uly"),
        P(None, "uly"),
        P("uly", None),
        P(),
    )
    out_specs = P(("blk", "uly"), None)
    nb, nz = mesh.shape["blk"], mesh.shape["uly"]
    run = body
    if HEADS == nb * nz:
        run = functools.partial(fused, nb, nz)
    return jax.shard_map(run, mesh=mesh, in_specs=in_specs, out_specs=out_specs, check_vma=False)
```

profile of v0, /device:TPU:0, one launch (start us, length us, event | category | flops | bytes accessed | tf_op | source)
XLA Modules:
  0.0 58.3 jit_solution(14979119539424021510)
XLA Ops:
  0.0 56.6 %shard_map.91 = bf16[48,2048]{1,0:T(8,128)(2,1)} custom-call(bf16[48,2048]{1,0:T(8,128)(2,1)} %tok_h.1, f32[1,2048]{1,0:T(1,128)} %bitcast.4, f32[1,2048]{1,0:T(1,128)} %bitcast.5, f32[1,2048]{1,0:T(1,128)} %bitcast.6, f32[1,32]{1,0:T(1,128)} %bitcast.7, bf16[2048,512]{1,0:T(8,128)(2,1)} %wq.1, bf16[2048,512]{1,0:T(8,128)(2,1)} %wk.1, bf16[2048,512]{1,0:T(8,128)(2,1)} %wv.1, ...), custom_call_target="tpu_custom_call" | custom-call | tf_op jit(solution)/shard_map/pallas_call | solution.py:250
  56.6 1.6 %copy.11 = bf16[48,2048]{1,0:T(8,128)(2,1)} copy(bf16[48,2048]{1,0:T(8,128)(2,1)} %shard_map.91) | data formatting | bytes 393216
where the time goes:
time: 58.4 us; the launch traced here: 58.3 us
  Pallas kernels  56.6 us (97%)
  local copies, waits for them, and re-layouts  1.62 us (3%)
    pallas_call x1, Pallas kernels, fused(): pl.pallas_call(functools.partial(kernel, nb, nz), out_shape=jax.ShapeDtyp...  56.6 us
    unnamed x1, local copies, waits for them, and re-layouts  1.62 us

commit v1 on v0

v1 whole, which is shorter than its diff:
```python
import functools
import math

import jax
import jax.numpy as jnp
from jax import lax
from jax.experimental import pallas as pl
from jax.experimental.pallas import tpu as pltpu
from jax.sharding import PartitionSpec as P

D = 2048
HEADS = 32
LOG2E = math.log2(math.e)
MESH = pl.DeviceIdType.MESH
SUB = 192


def kernel(
    nb, tok_h, shift_h, scale_h, gate_h, gain_h, wq, wk, wv, wo, out,
    tok, shift, scale, gate, gain, mod, wq_v, wk_v, wv_v, wo_v, kv_s, q_s, kv_r, q_r, top_v, sum_v, acc_v,
    att_s, att_r, part_v, part_s, pair_r, near_r, far_r,
    wsem, gs, gr, fs, hs, hr, bs, br, rs, rr,
):
    width = D // HEADS
    rows = tok.shape[0]
    span = nb * rows
    chunks = mod.shape[1]
    deep = mod.shape[3]
    tile = part_s.shape[-1]
    parts = D // tile
    mb, mz = lax.axis_index("blk"), lax.axis_index("uly")
    high = mz // 2
    middle = (mz + 1) // 2 == 1
    near = mz + 1 - 2 * lax.rem(mz, 2)
    inner = 2 - high
    outer = 3 - 3 * high

    barrier = pltpu.get_barrier_semaphore()
    for z in (inner, near):
        pl.semaphore_signal(barrier, inc=1, device_id={"uly": z}, device_id_type=MESH)

    @pl.when(middle)
    def _():
        pl.semaphore_signal(barrier, inc=1, device_id={"uly": outer}, device_id_type=MESH)

    for j in range(1, nb):
        pl.semaphore_signal(barrier, inc=1, device_id={"blk": lax.rem(mb + j, nb)}, device_id_type=MESH)

    pairs = (
        (tok_h, tok), (shift_h, shift), (scale_h, scale), (wk, wk_v), (wv, wv_v), (wq, wq_v),
        (wo, wo_v), (gate_h, gate), (gain_h, gain),
    )
    loads = [
        pltpu.make_async_copy(src, dst, wsem.at[i])
        for i, (src, dst) in enumerate(pairs)
    ]
    for load in loads:
        load.start()
    for load in loads[:3]:
        load.wait()

    values = tok[...].astype(jnp.float32)
    center = values - jnp.mean(values, axis=-1, keepdims=True)
    spread = jnp.mean(center * center, axis=-1, keepdims=True)
    normed = center * lax.rsqrt(spread + 1e-06)
    modded = (normed * (1.0 + scale[...]) + shift[...]).astype(jnp.bfloat16)
    for c in range(chunks):
        mod[0, c] = modded[:, c * deep : (c + 1) * deep]

    pl.semaphore_wait(barrier, nb + 1 + middle.astype(jnp.int32))

    def gather(way, c):
        slot = 1 if way == 0 else 3 - middle.astype(jnp.int32)
        return pltpu.make_async_remote_copy(
            src_ref=mod.at[0, c], dst_ref=mod.at[slot, c], send_sem=gs.at[way, c], recv_sem=gr.at[slot, c],
            device_id={"uly": inner if way else near}, device_id_type=MESH)

    def landed(k, c):
        return pltpu.make_async_remote_copy(
            src_ref=mod.at[0, c], dst_ref=mod.at[k, c], send_sem=gs.at[0, c], recv_sem=gr.at[k, c],
            device_id={"uly": near}, device_id_type=MESH)

    def forward(k, c):
        return pltpu.make_async_remote_copy(
            src_ref=mod.at[k, c], dst_ref=mod.at[k, c], send_sem=fs.at[k, c], recv_sem=gr.at[k, c],
            device_id={"uly": near}, device_id_type=MESH)

    @pl.when(middle)
    def _():
        for c in range(chunks):
            for way in (0, 1):
                gather(way, c).start()

    @pl.when(jnp.logical_not(middle))
    def _():
        for way in (0, 1):
            for c in range(chunks):
                gather(way, c).start()

    for load in loads[3:6]:
        load.wait()

    def place(k, b):
        return pl.ds(pl.multiple_of(k * span + b * rows, rows), rows)

    def heads_to(k, kind, b):
        src, dst = ((kv_s, kv_r), (q_s, q_r))[kind]
        return pltpu.make_async_remote_copy(
            src_ref=src.at[k, b], dst_ref=dst.at[place(k, mb), :], send_sem=hs.at[k, kind, b],
            recv_sem=hr.at[k, kind, mb], device_id={"blk": b}, device_id_type=MESH)

    def heads_from(k, kind, b):
        src, dst = ((kv_s, kv_r), (q_s, q_r))[kind]
        return pltpu.make_async_remote_copy(
            src_ref=src.at[k, b], dst_ref=dst.at[place(k, b), :], send_sem=hs.at[k, kind, b],
            recv_sem=hr.at[k, kind, b], device_id={"blk": b}, device_id_type=MESH)

    loads[8].wait()
    chosen = lax.broadcasted_iota(jnp.int32, gain.shape, 1) == mz * nb + mb
    factor = jnp.sum(jnp.where(chosen, gain[...], 0.0), axis=-1, keepdims=True) * (LOG2E / math.sqrt(width))

    def await_heads(k, kind):
        for j in range(1, nb):
            heads_from(k, kind, lax.rem(mb + j, nb)).wait_recv()

    def begin(start, size, first, last):
        where = pl.ds(pl.multiple_of(start, rows), size)
        kv = kv_r[first * span : last * span, :]
        scores = lax.dot_general(q_r[where, :], kv, (((1,), (1,)), ((), ())), preferred_element_type=jnp.float32)
        top = jnp.max(scores, axis=-1, keepdims=True)
        expo = jnp.exp2((scores - top) * factor)
        total = jnp.sum(expo, axis=-1, keepdims=True)
        summed = jnp.dot(expo.astype(jnp.bfloat16), kv, preferred_element_type=jnp.float32)
        return top, total, summed

    def keep(start, size, first, last):
        where = pl.ds(pl.multiple_of(start, rows), size)
        top_v[where, :], sum_v[where, :], acc_v[where, :] = begin(start, size, first, last)

    def more(start, size, first, last):
        where = pl.ds(pl.multiple_of(start, rows), size)
        kv = kv_r[first * span : last * span, :]
        scores = lax.dot_general(q_r[where, :], kv, (((1,), (1,)), ((), ())), preferred_element_type=jnp.float32)
        old = top_v[where, :]
        top = jnp.maximum(old, jnp.max(scores, axis=-1, keepdims=True))
        shrink = jnp.exp2((old - top) * factor)
        expo = jnp.exp2((scores - top) * factor)
        total = sum_v[where, :] * shrink + jnp.sum(expo, axis=-1, keepdims=True)
        summed = jnp.dot(expo.astype(jnp.bfloat16), kv, preferred_element_type=jnp.float32)
        return total, acc_v[where, :] * shrink + summed

    def first_attend():
        for k in (0, 1):
            await_heads(k, 0)
            await_heads(k, 1)

        def step(i, carry):
            keep(i * SUB, SUB, 0, 2)
            return carry

        lax.fori_loop(0, 2 * span // SUB, step, 0)

    def piece(k, carry):
        @pl.when((k == 3) & jnp.logical_not(middle))
        def _():
            first_attend()

        query = key = value = None
        for c in range(chunks):
            @pl.when((k > 0) & (jnp.logical_not(middle) | (k == 1)))
            def _():
                landed(k, c).wait_recv()

            @pl.when(middle & (k > 0) & (k < 3))
            def _():
                landed(k + 1, c).wait_recv()
                forward(k + 1, c).start()

            x = mod[k, c]
            deeps = slice(c * deep, (c + 1) * deep)
            more_k = jnp.dot(x, wk_v[deeps, :], preferred_element_type=jnp.float32)
            more_v = jnp.dot(x, wv_v[deeps, :], preferred_element_type=jnp.float32)
            more_q = jnp.dot(x, wq_v[deeps, :], preferred_element_type=jnp.float32)
            key = more_k if c == 0 else key + more_k
            value = more_v if c == 0 else value + more_v
            query = more_q if c == 0 else query + more_q

        def unit(part):
            power = jnp.mean(part * part, axis=-1, keepdims=True)
            return part * lax.rsqrt(power + 1e-06)

        def send(kind):
            def one(j, carry):
                heads_to(k, kind, lax.rem(mb + j, nb)).start()
                return carry

            lax.fori_loop(1, nb, one, 0)

        for h in range(nb):
            cols = slice(h * width, (h + 1) * width)
            kv_s[k, h] = jnp.concatenate([unit(key[:, cols]), value[:, cols]], axis=1).astype(jnp.bfloat16)
        send(0)
        kv_r[place(k, mb), :] = kv_s[k, mb]
        for h in range(nb):
            cols = slice(h * width, (h + 1) * width)
            line = unit(query[:, cols])
            q_s[k, h] = jnp.concatenate([line, jnp.zeros_like(line)], axis=1).astype(jnp.bfloat16)
        send(1)
        q_r[place(k, mb), :] = q_s[k, mb]
        return carry

    lax.fori_loop(0, 4, piece, 0)

    @pl.when(middle)
    def _():
        first_attend()

    await_heads(2, 0)
    await_heads(2, 1)

    def step(i, carry):
        keep(2 * span + i * SUB, SUB, 0, 3)
        return carry

    lax.fori_loop(0, span // SUB, step, 0)
    await_heads(3, 0)

    def back_to(k, b):
        return pltpu.make_async_remote_copy(
            src_ref=att_s.at[k, pl.ds(pl.multiple_of(b * rows, rows), rows), :], dst_ref=att_r.at[k, mb],
            send_sem=bs.at[k, b], recv_sem=br.at[k, mb], device_id={"blk": b}, device_id_type=MESH)

    def back_from(k, b):
        return pltpu.make_async_remote_copy(
            src_ref=att_s.at[k, pl.ds(pl.multiple_of(b * rows, rows), rows), :], dst_ref=att_r.at[k, b],
            send_sem=bs.at[k, b], recv_sem=br.at[k, b], device_id={"blk": b}, device_id_type=MESH)

    def finish(k):
        def step(i, carry):
            if k == 3:
                unused, total, summed = begin(k * span + i * SUB, SUB, 0, 4)
            else:
                total, summed = more(k * span + i * SUB, SUB, 3 if k == 2 else 2, 4)
            att_s[k, pl.ds(pl.multiple_of(i * SUB, rows), SUB), :] = (summed / total).astype(jnp.bfloat16)
            return carry

        lax.fori_loop(0, span // SUB, step, 0)

        def one(j, carry):
            back_to(k, lax.rem(mb + j, nb)).start()
            return carry

        lax.fori_loop(1, nb, one, 0)
        att_r[k, mb] = att_s[k, pl.ds(pl.multiple_of(mb * rows, rows), rows), :]

    def near_to(n):
        return pltpu.make_async_remote_copy(
            src_ref=part_s.at[1, n], dst_ref=near_r.at[n], send_sem=rs.at[1, n], recv_sem=rr.at[1, n],
            device_id={"uly": near}, device_id_type=MESH)

    def pair_to(k, n):
        return pltpu.make_async_remote_copy(
            src_ref=part_s.at[k, n], dst_ref=pair_r.at[k - 2, n], send_sem=rs.at[k, n], recv_sem=rr.at[k, n],
            device_id={"uly": near}, device_id_type=MESH)

    def far_to(k, n):
        return pltpu.make_async_remote_copy(
            src_ref=part_s.at[k, n], dst_ref=far_r.at[n], send_sem=rs.at[k, n], recv_sem=rr.at[0, n],
            device_id={"uly": inner if k == 2 else outer}, device_id_type=MESH)

    def project(k):
        for j in range(1, nb):
            back_from(k, lax.rem(mb + j, nb)).wait_recv()
        attended = jnp.concatenate([att_r[k, h][:, width:] for h in range(nb)], axis=1)
        for n in range(parts):
            part = jnp.dot(attended, wo_v[:, n * tile : (n + 1) * tile], preferred_element_type=jnp.float32)
            if k == 1:
                part_s[1, n] = part.astype(jnp.bfloat16)
                near_to(n).start()
            elif k == 0:
                part_v[0, n] = part
            else:
                @pl.when(middle)
                def _():
                    part_v[k, n] = part

                @pl.when(jnp.logical_not(middle))
                def _():
                    part_s[k, n] = part.astype(jnp.bfloat16)
                    pair_to(k, n).start()

    finish(2)
    await_heads(3, 1)
    finish(3)
    loads[6].wait()
    loads[7].wait()
    project(2)
    finish(1)
    project(3)
    finish(0)
    project(1)
    project(0)

    @pl.when(middle)
    def _():
        for k in (2, 3):
            for n in range(parts):
                pair_to(k, n).wait_recv()
                part_s[k, n] = (part_v[k, n] + pair_r[k - 2, n].astype(jnp.float32)).astype(jnp.bfloat16)
                far_to(k, n).start()

    for n in range(parts):
        far_to(2, n).wait_recv()
        near_to(n).wait_recv()
        total = part_v[0, n] + near_r[n].astype(jnp.float32) + far_r[n].astype(jnp.float32)
        cols = slice(n * tile, (n + 1) * tile)
        out[:, cols] = (tok[:, cols].astype(jnp.float32) + gate[:, cols] * total).astype(jnp.bfloat16)

    for way in (0, 1):
        for c in range(chunks):
            gather(way, c).wait_send()

    @pl.when(middle)
    def _():
        for k in (2, 3):
            for c in range(chunks):
                forward(k, c).wait_send()

    def sent(i, carry):
        b = lax.rem(mb + 1 + lax.rem(i, nb - 1), nb)
        k = i // (nb - 1)
        heads_to(k, 0, b).wait_send()
        heads_to(k, 1, b).wait_send()
        back_to(k, b).wait_send()
        return carry

    lax.fori_loop(0, 4 * (nb - 1), sent, 0)
    for k in (1, 2, 3):
        for n in range(parts):
            near_to(n).wait_send() if k == 1 else pair_to(k, n).wait_send()


def fused(nb, tokens, mod_shift, mod_scale, mod_gate, w_query, w_key, w_value, w_out, score_gain):
    rows = tokens.shape[0]
    cols = w_query.shape[1]
    chunks = 4
    tile = 512
    parts = D // tile
    span = nb * rows
    bf16, f32 = jnp.bfloat16, jnp.float32
    vmem = pl.BlockSpec(memory_space=pltpu.VMEM)
    hbm = pl.BlockSpec(memory_space=pltpu.HBM)
    dma = pltpu.SemaphoreType.DMA
    return pl.pallas_call(
        functools.partial(kernel, nb),
        out_shape=jax.ShapeDtypeStruct((rows, D), bf16),
        in_specs=[hbm] * 9,
        out_specs=vmem,
        scratch_shapes=[
            pltpu.VMEM((rows, D), bf16),
            pltpu.VMEM((1, D), f32),
            pltpu.VMEM((1, D), f32),
            pltpu.VMEM((1, D), f32),
            pltpu.VMEM((1, HEADS), f32),
            pltpu.VMEM((4, chunks, rows, D // chunks), bf16),
            pltpu.VMEM((D, cols), bf16),
            pltpu.VMEM((D, cols), bf16),
            pltpu.VMEM((D, cols), bf16),
            pltpu.VMEM((cols, D), bf16),
            pltpu.VMEM((4, nb, rows, 128), bf16),
            pltpu.VMEM((4, nb, rows, 128), bf16),
            pltpu.VMEM((4 * span, 128), bf16),
            pltpu.VMEM((4 * span, 128), bf16),
            pltpu.VMEM((4 * span, 1), f32),
            pltpu.VMEM((4 * span, 1), f32),
            pltpu.VMEM((4 * span, 128), f32),
            pltpu.VMEM((4, span, 128), bf16),
            pltpu.VMEM((4, nb, rows, 128), bf16),
            pltpu.VMEM((4, parts, rows, tile), f32),
            pltpu.VMEM((4, parts, rows, tile), bf16),
            pltpu.VMEM((2, parts, rows, tile), bf16),
            pltpu.VMEM((parts, rows, tile), bf16),
            pltpu.VMEM((parts, rows, tile), bf16),
            dma((9,)),
            dma((2, chunks)),
            dma((4, chunks)),
            dma((4, chunks)),
            dma((4, 2, nb)),
            dma((4, 2, nb)),
            dma((4, nb)),
            dma((4, nb)),
            dma((4, parts)),
            dma((4, parts)),
        ],
        compiler_params=pltpu.CompilerParams(
            collective_id=0, has_side_effects=True, vmem_limit_bytes=56 * 1024 * 1024
        ),
    )(
        tokens, mod_shift[None], mod_scale[None], mod_gate[None], score_gain[None],
        w_query, w_key, w_value, w_out,
    )


def modulate(tokens, mod_shift, mod_scale):
    values = tokens.astype(jnp.float32)
    center = values - jnp.mean(values, axis=-1, keepdims=True)
    spread = jnp.mean(center * center, axis=-1, keepdims=True)
    normed = center * lax.rsqrt(spread + 1e-06)
    return (normed * (1.0 + mod_scale) + mod_shift).astype(jnp.bfloat16)


def head_norm(projected, width):
    count = projected.shape[0]
    split = projected.reshape(count, -1, width)
    power = jnp.mean(split * split, axis=-1, keepdims=True)
    return (split * lax.rsqrt(power + 1e-06)).reshape(count, -1).astype(jnp.bfloat16)


def body(tokens, mod_shift, mod_scale, mod_gate, w_query, w_key, w_value, w_out, score_gain):
    width = D // HEADS
    local_cols = w_query.shape[1]
    local_heads = local_cols // width
    modded = modulate(tokens, mod_shift, mod_scale)
    piece = lax.all_gather(modded, "uly", axis=0, tiled=True)
    joined = jnp.concatenate(
        [
            jnp.dot(piece, w_query, preferred_element_type=jnp.float32),
            jnp.dot(piece, w_key, preferred_element_type=jnp.float32),
            jnp.dot(piece, w_value, preferred_element_type=jnp.float32),
        ],
        axis=1,
    )
    queries = head_norm(joined[:, :local_cols], width)
    keys = head_norm(joined[:, local_cols : 2 * local_cols], width)
    values = joined[:, 2 * local_cols :].astype(jnp.bfloat16)
    gains = lax.dynamic_slice_in_dim(score_gain, lax.axis_index("uly") * local_heads, local_heads)
    factors = gains / math.sqrt(width)
    rows = queries.shape[0]
    query_heads = queries.reshape(rows, local_heads, width)
    initial = (
        jnp.full((local_heads, rows), -jnp.inf, jnp.float32),
        jnp.zeros((local_heads, rows), jnp.float32),
        jnp.zeros((local_heads, rows, width), jnp.float32),
    )
    key_piece = lax.all_gather(keys, "blk", axis=0, tiled=True)
    value_piece = lax.all_gather(values, "blk", axis=0, tiled=True)
    count = key_piece.shape[0]
    groups = count // rows
    limit = max(rows, 1024)
    depth = max(
        [step for step in range(1, groups + 1) if groups % step == 0 and step * rows <= limit]
    )
    stride = depth * rows
    key_blocks = key_piece.reshape(count // stride, stride, local_heads, width)
    value_blocks = value_piece.reshape(count // stride, stride, local_heads, width)

    def one_block(carry, blocks):
        run_max, run_total, run_acc = carry
        key_block, value_block = blocks
        scores = jnp.einsum(
            "rhd,khd->hrk", query_heads, key_block, preferred_element_type=jnp.float32
        )
        scores = scores * factors[:, None, None]
        new_max = jnp.maximum(run_max, jnp.max(scores, axis=-1))
        expo = jnp.exp(scores - new_max[..., None])
        rescale = jnp.exp(run_max - new_max)
        new_total = run_total * rescale + jnp.sum(expo, axis=-1)
        summed = jnp.einsum(
            "hrk,khd->hrd",
            expo.astype(jnp.bfloat16),
            value_block,
            preferred_element_type=jnp.float32,
        )
        new_acc = run_acc * rescale[..., None] + summed
        return ((new_max, new_total, new_acc), None)

    result, unused = lax.scan(one_block, initial, (key_blocks, value_blocks))
    run_max, run_total, run_acc = result
    attended = (run_acc / run_total[..., None]).astype(jnp.bfloat16)
    attended = attended.transpose(1, 0, 2).reshape(rows, local_cols)
    returned = lax.all_to_all(attended, "uly", split_axis=0, concat_axis=1, tiled=True)
    projected = jnp.dot(
        returned,
        lax.all_gather(w_out, "uly", axis=0, tiled=True),
        preferred_element_type=jnp.float32,
    )
    return (tokens.astype(jnp.float32) + mod_gate * projected).astype(jnp.bfloat16)


def solution(mesh):
    in_specs = (
        P(("blk", "uly"), None),
        P(),
        P(),
        P(),
        P(None, "uly"),
        P(None, "uly"),
        P(None, "uly"),
        P("uly", None),
        P(),
    )
    out_specs = P(("blk", "uly"), None)
    nb, nz = mesh.shape["blk"], mesh.shape["uly"]
    run = body
    if HEADS == nb * nz and nz == 4:
        run = functools.partial(fused, nb)
    return jax.shard_map(run, mesh=mesh, in_specs=in_specs, out_specs=out_specs, check_vma=False)
```

time: 58.4 us -> 53.8 us (0.921)
  Pallas kernels: 56.6 us -> 52 us
    pallas_call x1, Pallas kernels: 56.6 us -> 52 us  [fused(): pl.pallas_call(functools.partial(kernel, nb), out_shape=jax.ShapeDtypeStr...]
where the time goes in v1:
time: 53.8 us; the launch traced here: 53.6 us
  Pallas kernels  52 us (97%)
  local copies, waits for them, and re-layouts  1.62 us (3%)
    pallas_call x1, Pallas kernels, fused(): pl.pallas_call(functools.partial(kernel, nb), out_shape=jax.ShapeDtypeStr...  52 us
    unnamed x1, local copies, waits for them, and re-layouts  1.62 us

profile of v1, /device:TPU:0, one launch (start us, length us, event | category | flops | bytes accessed | tf_op | source)
XLA Modules:
  0.0 53.6 jit_solution(1985198403108983258)
XLA Ops:
  0.0 52.0 %shard_map.91 = bf16[48,2048]{1,0:T(8,128)(2,1)} custom-call(bf16[48,2048]{1,0:T(8,128)(2,1)} %tok_h.1, f32[1,2048]{1,0:T(1,128)} %bitcast.4, f32[1,2048]{1,0:T(1,128)} %bitcast.5, f32[1,2048]{1,0:T(1,128)} %bitcast.6, f32[1,32]{1,0:T(1,128)} %bitcast.7, bf16[2048,512]{1,0:T(8,128)(2,1)} %wq.1, bf16[2048,512]{1,0:T(8,128)(2,1)} %wk.1, bf16[2048,512]{1,0:T(8,128)(2,1)} %wv.1, ...), custom_call_target="tpu_custom_call" | custom-call | tf_op jit(solution)/shard_map/pallas_call | solution.py:354
  52.0 1.6 %copy.11 = bf16[48,2048]{1,0:T(8,128)(2,1)} copy(bf16[48,2048]{1,0:T(8,128)(2,1)} %shard_map.91) | data formatting | bytes 393216

commit v2 on v1

--- a/solution.py
+++ b/solution.py
@@ -12,12 +12,12 @@
 HEADS = 32
 LOG2E = math.log2(math.e)
 MESH = pl.DeviceIdType.MESH
-SUB = 192
+SUB = 384
 
 
 def kernel(
     nb, tok_h, shift_h, scale_h, gate_h, gain_h, wq, wk, wv, wo, out,
-    tok, shift, scale, gate, gain, mod, wq_v, wk_v, wv_v, wo_v, kv_s, q_s, kv_r, q_r, top_v, sum_v, acc_v,
+    tok, shift, scale, gate, gain, mod, wq_v, wk_v, wv_v, wo_v, kv_s, q_s, kv_r, q_r, vt, top_v, sum_v, acc_v,
     att_s, att_r, part_v, part_s, pair_r, near_r, far_r,
     wsem, gs, gr, fs, hs, hr, bs, br, rs, rr,
 ):
@@ -123,42 +123,45 @@
         for j in range(1, nb):
             heads_from(k, kind, lax.rem(mb + j, nb)).wait_recv()
 
-    def begin(start, size, first, last):
-        where = pl.ds(pl.multiple_of(start, rows), size)
-        kv = kv_r[first * span : last * span, :]
-        scores = lax.dot_general(q_r[where, :], kv, (((1,), (1,)), ((), ())), preferred_element_type=jnp.float32)
-        top = jnp.max(scores, axis=-1, keepdims=True)
+    def flip(k):
+        vt[:, k * span : (k + 1) * span] = kv_r[k * span : (k + 1) * span, :].T[width:, :]
+
+    def scored(k, c, first, last):
+        q = q_r[k * span + c * SUB : k * span + (c + 1) * SUB, :]
+        return lax.dot_general(
+            kv_r[first * span : last * span, :], q, (((1,), (1,)), ((), ())), preferred_element_type=jnp.float32)
+
+    def begin(k, c, first, last):
+        scores = scored(k, c, first, last)
+        top = jnp.max(scores, axis=0, keepdims=True)
         expo = jnp.exp2((scores - top) * factor)
-        total = jnp.sum(expo, axis=-1, keepdims=True)
-        summed = jnp.dot(expo.astype(jnp.bfloat16), kv, preferred_element_type=jnp.float32)
+        total = jnp.sum(expo, axis=0, keepdims=True)
+        summed = jnp.dot(vt[:, first * span : last * span], expo.astype(jnp.bfloat16), preferred_element_type=jnp.float32)
         return top, total, summed
 
-    def keep(start, size, first, last):
-        where = pl.ds(pl.multiple_of(start, rows), size)
-        top_v[where, :], sum_v[where, :], acc_v[where, :] = begin(start, size, first, last)
-
-    def more(start, size, first, last):
-        where = pl.ds(pl.multiple_of(start, rows), size)
-        kv = kv_r[first * span : last * span, :]
-        scores = lax.dot_general(q_r[where, :], kv, (((1,), (1,)), ((), ())), preferred_element_type=jnp.float32)
-        old = top_v[where, :]
-        top = jnp.maximum(old, jnp.max(scores, axis=-1, keepdims=True))
+    def keep(k, first, last):
+        for c in range(span // SUB):
+            cols = slice(c * SUB, (c + 1) * SUB)
+            top_v[k, :, cols], sum_v[k, :, cols], acc_v[k, :, cols] = begin(k, c, first, last)
+
+    def more(k, c, first, last):
+        cols = slice(c * SUB, (c + 1) * SUB)
+        scores = scored(k, c, first, last)
+        old = top_v[k, :, cols]
+        top = jnp.maximum(old, jnp.max(scores, axis=0, keepdims=True))
         shrink = jnp.exp2((old - top) * factor)
         expo = jnp.exp2((scores - top) * factor)
-        total = sum_v[where, :] * shrink + jnp.sum(expo, axis=-1, keepdims=True)
-        summed = jnp.dot(expo.astype(jnp.bfloat16), kv, preferred_element_type=jnp.float32)
-        return total, acc_v[where, :] * shrink + summed
+        total = sum_v[k, :, cols] * shrink + jnp.sum(expo, axis=0, keepdims=True)
+        summed = jnp.dot(vt[:, first * span : last * span], expo.astype(jnp.bfloat16), preferred_element_type=jnp.float32)
+        return total, acc_v[k, :, cols] * shrink + summed
 
     def first_attend():
         for k in (0, 1):
             await_heads(k, 0)
             await_heads(k, 1)
-
-        def step(i, carry):
-            keep(i * SUB, SUB, 0, 2)
-            return carry
-
-        lax.fori_loop(0, 2 * span // SUB, step, 0)
+            flip(k)
+        for k in (0, 1):
+            keep(k, 0, 2)
 
     def piece(k, carry):
         @pl.when((k == 3) & jnp.logical_not(middle))
@@ -217,41 +220,46 @@
 
     await_heads(2, 0)
     await_heads(2, 1)
-
-    def step(i, carry):
-        keep(2 * span + i * SUB, SUB, 0, 3)
-        return carry
-
-    lax.fori_loop(0, span // SUB, step, 0)
+    flip(2)
+    keep(2, 0, 3)
     await_heads(3, 0)
-
-    def back_to(k, b):
-        return pltpu.make_async_remote_copy(
-            src_ref=att_s.at[k, pl.ds(pl.multiple_of(b * rows, rows), rows), :], dst_ref=att_r.at[k, mb],
-            send_sem=bs.at[k, b], recv_sem=br.at[k, mb], device_id={"blk": b}, device_id_type=MESH)
-
-    def back_from(k, b):
-        return pltpu.make_async_remote_copy(
-            src_ref=att_s.at[k, pl.ds(pl.multiple_of(b * rows, rows), rows), :], dst_ref=att_r.at[k, b],
-            send_sem=bs.at[k, b], recv_sem=br.at[k, b], device_id={"blk": b}, device_id_type=MESH)
-
-    def finish(k):
-        def step(i, carry):
-            if k == 3:
-                unused, total, summed = begin(k * span + i * SUB, SUB, 0, 4)
-            else:
-                total, summed = more(k * span + i * SUB, SUB, 3 if k == 2 else 2, 4)
-            att_s[k, pl.ds(pl.multiple_of(i * SUB, rows), SUB), :] = (summed / total).astype(jnp.bfloat16)
+    flip(3)
+
+    def back_to(j, b):
+        return pltpu.make_async_remote_copy(
+            src_ref=att_s.at[j, pl.ds(pl.multiple_of(b * rows, rows), rows), :], dst_ref=att_r.at[j, mb],
+            send_sem=bs.at[j, b], recv_sem=br.at[j, mb], device_id={"blk": b}, device_id_type=MESH)
+
+    def back_from(j, b):
+        return pltpu.make_async_remote_copy(
+            src_ref=att_s.at[j, pl.ds(pl.multiple_of(b * rows, rows), rows), :], dst_ref=att_r.at[j, b],
+            send_sem=bs.at[j, b], recv_sem=br.at[j, b], device_id={"blk": b}, device_id_type=MESH)
+
+    def finished(k, c):
+        if k == 3:
+            unused, total, summed = begin(k, c, 0, 4)
+        else:
+            total, summed = more(k, c, 3 if k == 2 else 2, 4)
+        return summed / total
+
+    def finish(j):
+        if j == 0:
+            lower = [finished(2, c) for c in range(span // SUB)]
+            await_heads(3, 1)
+            upper = [finished(3, c) for c in range(span // SUB)]
+        else:
+            lower = [finished(1, c) for c in range(span // SUB)]
+            upper = [finished(0, c) for c in range(span // SUB)]
+        for c in range(span // SUB):
+            both = jnp.concatenate([lower[c], upper[c]], axis=0)
+            att_s[j, c * SUB : (c + 1) * SUB, :] = both.T.astype(jnp.bfloat16)
+
+        def one(i, carry):
+            back_to(j, lax.rem(mb + i, nb)).start()
             return carry
 
-        lax.fori_loop(0, span // SUB, step, 0)
-
-        def one(j, carry):
-            back_to(k, lax.rem(mb + j, nb)).start()
-            return carry
-
         lax.fori_loop(1, nb, one, 0)
-        att_r[k, mb] = att_s[k, pl.ds(pl.multiple_of(mb * rows, rows), rows), :]
+        att_r[j, mb] = att_s[j, pl.ds(pl.multiple_of(mb * rows, rows), rows), :]
 
     def near_to(n):
         return pltpu.make_async_remote_copy(
@@ -268,43 +276,45 @@
             src_ref=part_s.at[k, n], dst_ref=far_r.at[n], send_sem=rs.at[k, n], recv_sem=rr.at[0, n],
             device_id={"uly": inner if k == 2 else outer}, device_id_type=MESH)
 
-    def project(k):
-        for j in range(1, nb):
-            back_from(k, lax.rem(mb + j, nb)).wait_recv()
-        attended = jnp.concatenate([att_r[k, h][:, width:] for h in range(nb)], axis=1)
+    def project(j):
+        for i in range(1, nb):
+            back_from(j, lax.rem(mb + i, nb)).wait_recv()
+        pieces = [att_r[j, h] for h in range(nb)]
+        attended = jnp.concatenate(
+            [
+                jnp.concatenate([one[:, :width] for one in pieces], axis=1),
+                jnp.concatenate([one[:, width:] for one in pieces], axis=1),
+            ],
+            axis=0,
+        )
         for n in range(parts):
             part = jnp.dot(attended, wo_v[:, n * tile : (n + 1) * tile], preferred_element_type=jnp.float32)
-            if k == 1:
-                part_s[1, n] = part.astype(jnp.bfloat16)
-                near_to(n).start()
-            elif k == 0:
-                part_v[0, n] = part
-            else:
-                @pl.when(middle)
-                def _():
-                    part_v[k, n] = part
+            if j == 0:
+                for k in (2, 3):
+                    mine = part[(k - 2) * rows : (k - 1) * rows]
+                    part_v[k, n] = mine
+                    part_s[k, n] = mine.astype(jnp.bfloat16)
 
                 @pl.when(jnp.logical_not(middle))
                 def _():
-                    part_s[k, n] = part.astype(jnp.bfloat16)
-                    pair_to(k, n).start()
-
-    finish(2)
-    await_heads(3, 1)
-    finish(3)
+                    for k in (2, 3):
+                        pair_to(k, n).start()
+            else:
+                part_s[1, n] = part[:rows].astype(jnp.bfloat16)
+                near_to(n).start()
+                part_v[0, n] = part[rows:]
+
+    finish(0)
+    finish(1)
     loads[6].wait()
     loads[7].wait()
-    project(2)
-    finish(1)
-    project(3)
-    finish(0)
+    project(0)
     project(1)
-    project(0)
 
     @pl.when(middle)
     def _():
-        for k in (2, 3):
-            for n in range(parts):
+        for n in range(parts):
+            for k in (2, 3):
                 pair_to(k, n).wait_recv()
                 part_s[k, n] = (part_v[k, n] + pair_r[k - 2, n].astype(jnp.float32)).astype(jnp.bfloat16)
                 far_to(k, n).start()
@@ -331,10 +341,12 @@
         k = i // (nb - 1)
         heads_to(k, 0, b).wait_send()
         heads_to(k, 1, b).wait_send()
-        back_to(k, b).wait_send()
         return carry
 
     lax.fori_loop(0, 4 * (nb - 1), sent, 0)
+    for j in (0, 1):
+        for i in range(1, nb):
+            back_to(j, lax.rem(mb + i, nb)).wait_send()
     for k in (1, 2, 3):
         for n in range(parts):
             near_to(n).wait_send() if k == 1 else pair_to(k, n).wait_send()
@@ -371,11 +383,12 @@
             pltpu.VMEM((4, nb, rows, 128), bf16),
             pltpu.VMEM((4 * span, 128), bf16),
             pltpu.VMEM((4 * span, 128), bf16),
-            pltpu.VMEM((4 * span, 1), f32),
-            pltpu.VMEM((4 * span, 1), f32),
-            pltpu.VMEM((4 * span, 128), f32),
-            pltpu.VMEM((4, span, 128), bf16),
-            pltpu.VMEM((4, nb, rows, 128), bf16),
+            pltpu.VMEM((64, 4 * span), bf16),
+            pltpu.VMEM((4, 1, span), f32),
+            pltpu.VMEM((4, 1, span), f32),
+            pltpu.VMEM((4, 64, span), f32),
+            pltpu.VMEM((2, span, 128), bf16),
+            pltpu.VMEM((2, nb, rows, 128), bf16),
             pltpu.VMEM((4, parts, rows, tile), f32),
             pltpu.VMEM((4, parts, rows, tile), bf16),
             pltpu.VMEM((2, parts, rows, tile), bf16),
@@ -387,8 +400,8 @@
             dma((4, chunks)),
             dma((4, 2, nb)),
             dma((4, 2, nb)),
-            dma((4, nb)),
-            dma((4, nb)),
+            dma((2, nb)),
+            dma((2, nb)),
             dma((4, parts)),
             dma((4, parts)),
         ],

time: 53.8 us -> 50.5 us (0.939)
  Pallas kernels: 52 us -> 48.7 us
    pallas_call x1, Pallas kernels: 52 us -> 48.7 us  [fused(): pl.pallas_call(functools.partial(kernel, nb), out_shape=jax.ShapeDtypeStr...]
where the time goes in v2:
time: 50.5 us; the launch traced here: 50.4 us
  Pallas kernels  48.7 us (96%)
  local copies, waits for them, and re-layouts  1.62 us (3%)
    pallas_call x1, Pallas kernels, fused(): pl.pallas_call(functools.partial(kernel, nb), out_shape=jax.ShapeDtypeStr...  48.7 us
    unnamed x1, local copies, waits for them, and re-layouts  1.62 us

profile of v2, /device:TPU:0, one launch (start us, length us, event | category | flops | bytes accessed | tf_op | source)
XLA Modules:
  0.0 50.4 jit_solution(3801137398121935253)
XLA Ops:
  0.0 48.7 %shard_map.91 = bf16[48,2048]{1,0:T(8,128)(2,1)} custom-call(bf16[48,2048]{1,0:T(8,128)(2,1)} %tok_h.1, f32[1,2048]{1,0:T(1,128)} %bitcast.4, f32[1,2048]{1,0:T(1,128)} %bitcast.5, f32[1,2048]{1,0:T(1,128)} %bitcast.6, f32[1,32]{1,0:T(1,128)} %bitcast.7, bf16[2048,512]{1,0:T(8,128)(2,1)} %wq.1, bf16[2048,512]{1,0:T(8,128)(2,1)} %wk.1, bf16[2048,512]{1,0:T(8,128)(2,1)} %wv.1, ...), custom_call_target="tpu_custom_call" | custom-call | tf_op jit(solution)/shard_map/pallas_call | solution.py:366
  48.8 1.6 %copy.11 = bf16[48,2048]{1,0:T(8,128)(2,1)} copy(bf16[48,2048]{1,0:T(8,128)(2,1)} %shard_map.91) | data formatting | bytes 393216

commit v3 on v2

--- a/solution.py
+++ b/solution.py
@@ -297,12 +297,16 @@
 
                 @pl.when(jnp.logical_not(middle))
                 def _():
-                    for k in (2, 3):
-                        pair_to(k, n).start()
+                    pair_to(3, n).start()
             else:
                 part_s[1, n] = part[:rows].astype(jnp.bfloat16)
                 near_to(n).start()
                 part_v[0, n] = part[rows:]
+        if j == 0:
+            @pl.when(jnp.logical_not(middle))
+            def _():
+                for n in range(parts):
+                    pair_to(2, n).start()
 
     finish(0)
     finish(1)
@@ -313,8 +317,8 @@
 
     @pl.when(middle)
     def _():
-        for n in range(parts):
-            for k in (2, 3):
+        for k in (3, 2):
+            for n in range(parts):
                 pair_to(k, n).wait_recv()
                 part_s[k, n] = (part_v[k, n] + pair_r[k - 2, n].astype(jnp.float32)).astype(jnp.bfloat16)
                 far_to(k, n).start()

time: 50.5 us -> 48.1 us (0.952)
  the two profiles are of different devices: /device:TPU:0 before, /device:TPU:16 now
where the time goes in v3:
time: 48.1 us; the launch traced here: 48 us
  Pallas kernels  46.3 us (96%)
  local copies, waits for them, and re-layouts  1.62 us (3%)
    pallas_call x1, Pallas kernels, fused(): pl.pallas_call(functools.partial(kernel, nb), out_shape=jax.ShapeDtypeStr...  46.3 us
    unnamed x1, local copies, waits for them, and re-layouts  1.62 us

profile of v3, /device:TPU:16, one launch (start us, length us, event | category | flops | bytes accessed | tf_op | source)
XLA Modules:
  0.0 48.0 jit_solution(2598079869259667613)
XLA Ops:
  0.0 46.3 %shard_map.91 = bf16[48,2048]{1,0:T(8,128)(2,1)} custom-call(bf16[48,2048]{1,0:T(8,128)(2,1)} %tok_h.1, f32[1,2048]{1,0:T(1,128)} %bitcast.4, f32[1,2048]{1,0:T(1,128)} %bitcast.5, f32[1,2048]{1,0:T(1,128)} %bitcast.6, f32[1,32]{1,0:T(1,128)} %bitcast.7, bf16[2048,512]{1,0:T(8,128)(2,1)} %wq.1, bf16[2048,512]{1,0:T(8,128)(2,1)} %wk.1, bf16[2048,512]{1,0:T(8,128)(2,1)} %wv.1, ...), custom_call_target="tpu_custom_call" | custom-call | tf_op jit(solution)/shard_map/pallas_call | solution.py:370
  46.4 1.6 %copy.11 = bf16[48,2048]{1,0:T(8,128)(2,1)} copy(bf16[48,2048]{1,0:T(8,128)(2,1)} %shard_map.91) | data formatting | bytes 393216

commit v4 on v3

--- a/solution.py
+++ b/solution.py
@@ -13,13 +13,14 @@
 LOG2E = math.log2(math.e)
 MESH = pl.DeviceIdType.MESH
 SUB = 384
+TWIN = 1024
 
 
 def kernel(
     nb, tok_h, shift_h, scale_h, gate_h, gain_h, wq, wk, wv, wo, out,
     tok, shift, scale, gate, gain, mod, wq_v, wk_v, wv_v, wo_v, kv_s, q_s, kv_r, q_r, vt, top_v, sum_v, acc_v,
-    att_s, att_r, part_v, part_s, pair_r, near_r, far_r,
-    wsem, gs, gr, fs, hs, hr, bs, br, rs, rr,
+    att_s, att_r, full_v, full_r, twin_v, part_v, part_s, pair_r, near_r, far_r,
+    wsem, gs, gr, fs, hs, hr, bs, br, rs, rr, es, er, ts, tr,
 ):
     width = D // HEADS
     rows = tok.shape[0]
@@ -28,6 +29,7 @@
     deep = mod.shape[3]
     tile = part_s.shape[-1]
     parts = D // tile
+    apart = parts - twin_v.shape[1] // tile
     mb, mz = lax.axis_index("blk"), lax.axis_index("uly")
     high = mz // 2
     middle = (mz + 1) // 2 == 1
@@ -103,6 +105,38 @@
     def place(k, b):
         return pl.ds(pl.multiple_of(k * span + b * rows, rows), rows)
 
+    depth = wo_v.shape[0] // nb
+    sibling = mb + 1 - 2 * lax.rem(mb, 2)
+
+    def slab(b):
+        return pl.ds(pl.multiple_of(b * depth, depth), depth)
+
+    def twin_out():
+        return pltpu.make_async_remote_copy(
+            src_ref=wo_v.at[slab(mb), apart * tile :], dst_ref=twin_v.at[slab(mb), :], send_sem=ts.at[0, 0],
+            recv_sem=tr.at[mb], device_id={"uly": near}, device_id_type=MESH)
+
+    def twin_in(b):
+        return pltpu.make_async_remote_copy(
+            src_ref=twin_v.at[slab(b), :], dst_ref=twin_v.at[slab(b), :], send_sem=ts.at[0, 0],
+            recv_sem=tr.at[b], device_id={"uly": near}, device_id_type=MESH)
+
+    def twin_share(j):
+        return pltpu.make_async_remote_copy(
+            src_ref=twin_v.at[slab(mb), :], dst_ref=twin_v.at[slab(mb), :], send_sem=ts.at[0, j],
+            recv_sem=tr.at[mb], device_id={"blk": sibling if j == 0 else lax.rem(mb + 2 * j, nb)}, device_id_type=MESH)
+
+    def twin_pass(j):
+        b = lax.rem(mb + 2 * j, nb)
+        return pltpu.make_async_remote_copy(
+            src_ref=twin_v.at[slab(b), :], dst_ref=twin_v.at[slab(b), :], send_sem=ts.at[1, j],
+            recv_sem=tr.at[b], device_id={"blk": sibling}, device_id_type=MESH)
+
+    def full_to(k):
+        return pltpu.make_async_remote_copy(
+            src_ref=full_v.at[k], dst_ref=full_r.at[k], send_sem=es.at[k], recv_sem=er.at[k],
+            device_id={"uly": near}, device_id_type=MESH)
+
     def heads_to(k, kind, b):
         src, dst = ((kv_s, kv_r), (q_s, q_r))[kind]
         return pltpu.make_async_remote_copy(
@@ -167,6 +201,11 @@
         @pl.when((k == 3) & jnp.logical_not(middle))
         def _():
             first_attend()
+
+        @pl.when((k == 1) & jnp.logical_not(middle))
+        def _():
+            loads[6].wait()
+            twin_out().start()
 
         query = key = value = None
         for c in range(chunks):
@@ -216,6 +255,11 @@
 
     @pl.when(middle)
     def _():
+        loads[6].wait()
+        twin_in(mb).wait_recv()
+        for j in range(1, nb // 2):
+            twin_share(j).start()
+        twin_share(0).start()
         first_attend()
 
     await_heads(2, 0)
@@ -287,7 +331,17 @@
             ],
             axis=0,
         )
-        for n in range(parts):
+        if j == 0:
+            full_v[2] = attended[:rows]
+            full_v[3] = attended[rows:]
+        else:
+            full_v[1] = attended[:rows]
+
+        @pl.when(jnp.logical_not(middle))
+        def _():
+            full_to(3 if j == 0 else 1).start()
+
+        for n in range(apart):
             part = jnp.dot(attended, wo_v[:, n * tile : (n + 1) * tile], preferred_element_type=jnp.float32)
             if j == 0:
                 for k in (2, 3):
@@ -305,30 +359,85 @@
         if j == 0:
             @pl.when(jnp.logical_not(middle))
             def _():
-                for n in range(parts):
+                full_to(2).start()
+                for n in range(apart):
                     pair_to(2, n).start()
+
+            @pl.when(middle)
+            def _():
+                for n in range(apart, parts):
+                    part = jnp.dot(attended, wo_v[:, n * tile : (n + 1) * tile], preferred_element_type=jnp.float32)
+                    for k in (2, 3):
+                        part_v[k, n] = part[(k - 2) * rows : (k - 1) * rows]
+        else:
+            for n in range(apart, parts):
+                part = jnp.dot(attended, wo_v[:, n * tile : (n + 1) * tile], preferred_element_type=jnp.float32)
+                part_s[1, n] = part[:rows].astype(jnp.bfloat16)
+
+                @pl.when(middle)
+                def _():
+                    near_to(n).start()
+
+                part_v[0, n] = part[rows:]
 
     finish(0)
     finish(1)
-    loads[6].wait()
+
+    @pl.when(middle)
+    def _():
+        for j in range(1, nb // 2):
+            twin_in(lax.rem(mb + 2 * j, nb)).wait_recv()
+            twin_pass(j).start()
+
     loads[7].wait()
     project(0)
     project(1)
 
+    def twin(k, n):
+        cols = slice((n - apart) * tile, (n - apart + 1) * tile)
+        return jnp.dot(full_r[k], twin_v[:, cols], preferred_element_type=jnp.float32)
+
     @pl.when(middle)
     def _():
+        twin_in(sibling).wait_recv()
+        for j in range(1, nb // 2):
+            twin_in(lax.rem(sibling + 2 * j, nb)).wait_recv()
         for k in (3, 2):
-            for n in range(parts):
+            full_to(k).wait_recv()
+            for n in range(apart, parts):
+                part_s[k, n] = (part_v[k, n] + twin(k, n)).astype(jnp.bfloat16)
+                far_to(k, n).start()
+            for n in range(apart):
                 pair_to(k, n).wait_recv()
                 part_s[k, n] = (part_v[k, n] + pair_r[k - 2, n].astype(jnp.float32)).astype(jnp.bfloat16)
                 far_to(k, n).start()
-
-    for n in range(parts):
+        full_to(1).wait_recv()
+        for n in range(apart, parts):
+            part_v[0, n] += twin(1, n)
+
+    def settle(n, extra):
+        total = part_v[0, n] + far_r[n].astype(jnp.float32)
+        if extra:
+            total = total + near_r[n].astype(jnp.float32)
+        cols = slice(n * tile, (n + 1) * tile)
+        out[:, cols] = (tok[:, cols].astype(jnp.float32) + gate[:, cols] * total).astype(jnp.bfloat16)
+
+    for n in range(apart, parts):
+        far_to(2, n).wait_recv()
+
+        @pl.when(middle)
+        def _():
+            settle(n, False)
+
+        @pl.when(jnp.logical_not(middle))
+        def _():
+            near_to(n).wait_recv()
+            settle(n, True)
+
+    for n in range(apart):
         far_to(2, n).wait_recv()
         near_to(n).wait_recv()
-        total = part_v[0, n] + near_r[n].astype(jnp.float32) + far_r[n].astype(jnp.float32)
-        cols = slice(n * tile, (n + 1) * tile)
-        out[:, cols] = (tok[:, cols].astype(jnp.float32) + gate[:, cols] * total).astype(jnp.bfloat16)
+        settle(n, True)
 
     for way in (0, 1):
         for c in range(chunks):
@@ -352,8 +461,24 @@
         for i in range(1, nb):
             back_to(j, lax.rem(mb + i, nb)).wait_send()
     for k in (1, 2, 3):
-        for n in range(parts):
+        for n in range(apart):
             near_to(n).wait_send() if k == 1 else pair_to(k, n).wait_send()
+
+    @pl.when(middle)
+    def _():
+        for k in (1, 2, 3):
+            for n in range(apart, parts):
+                near_to(n).wait_send() if k == 1 else pair_to(k, n).wait_send()
+        for j in range(nb // 2):
+            twin_share(j).wait_send()
+        for j in range(1, nb // 2):
+            twin_pass(j).wait_send()
+
+    @pl.when(jnp.logical_not(middle))
+    def _():
+        twin_out().wait_send()
+        for k in (1, 2, 3):
+            full_to(k).wait_send()
 
 
 def fused(nb, tokens, mod_shift, mod_scale, mod_gate, w_query, w_key, w_value, w_out, score_gain):
@@ -393,6 +518,9 @@
             pltpu.VMEM((4, 64, span), f32),
             pltpu.VMEM((2, span, 128), bf16),
             pltpu.VMEM((2, nb, rows, 128), bf16),
+            pltpu.VMEM((4, rows, cols), bf16),
+            pltpu.VMEM((4, rows, cols), bf16),
+            pltpu.VMEM((cols, TWIN), bf16),
             pltpu.VMEM((4, parts, rows, tile), f32),
             pltpu.VMEM((4, parts, rows, tile), bf16),
             pltpu.VMEM((2, parts, rows, tile), bf16),
@@ -408,6 +536,10 @@
             dma((2, nb)),
             dma((4, parts)),
             dma((4, parts)),
+            dma((4,)),
+            dma((4,)),
+            dma((2, nb // 2)),
+            dma((nb,)),
         ],
         compiler_params=pltpu.CompilerParams(
             collective_id=0, has_side_effects=True, vmem_limit_bytes=56 * 1024 * 1024
@@ -519,6 +651,6 @@
     out_specs = P(("blk", "uly"), None)
     nb, nz = mesh.shape["blk"], mesh.shape["uly"]
     run = body
-    if HEADS == nb * nz and nz == 4:
+    if HEADS == nb * nz and nz == 4 and nb % 2 == 0:
         run = functools.partial(fused, nb)
     return jax.shard_map(run, mesh=mesh, in_specs=in_specs, out_specs=out_specs, check_vma=False)

time: 48.1 us -> 47.5 us (0.988)
  the two profiles are of different devices: /device:TPU:16 before, /device:TPU:0 now
where the time goes in v4:
time: 47.5 us; the launch traced here: 47.3 us
  Pallas kernels  45.7 us (96%)
  local copies, waits for them, and re-layouts  1.62 us (3%)
    pallas_call x1, Pallas kernels, fused(): pl.pallas_call(functools.partial(kernel, nb), out_shape=jax.ShapeDtypeStr...  45.7 us
    unnamed x1, local copies, waits for them, and re-layouts  1.62 us

profile of v4, /device:TPU:0, one launch (start us, length us, event | category | flops | bytes accessed | tf_op | source)
XLA Modules:
  0.0 47.3 jit_solution(8940447533038988079)
XLA Ops:
  0.0 45.7 %shard_map.91 = bf16[48,2048]{1,0:T(8,128)(2,1)} custom-call(bf16[48,2048]{1,0:T(8,128)(2,1)} %tok_h.1, f32[1,2048]{1,0:T(1,128)} %bitcast.4, f32[1,2048]{1,0:T(1,128)} %bitcast.5, f32[1,2048]{1,0:T(1,128)} %bitcast.6, f32[1,32]{1,0:T(1,128)} %bitcast.7, bf16[2048,512]{1,0:T(8,128)(2,1)} %wq.1, bf16[2048,512]{1,0:T(8,128)(2,1)} %wk.1, bf16[2048,512]{1,0:T(8,128)(2,1)} %wv.1, ...), custom_call_target="tpu_custom_call" | custom-call | tf_op jit(solution)/shard_map/pallas_call | solution.py:495
  45.7 1.6 %copy.11 = bf16[48,2048]{1,0:T(8,128)(2,1)} copy(bf16[48,2048]{1,0:T(8,128)(2,1)} %shard_map.91) | data formatting | bytes 393216

commit v5 on v4

--- a/solution.py
+++ b/solution.py
@@ -72,7 +72,7 @@
     pl.semaphore_wait(barrier, nb + 1 + middle.astype(jnp.int32))
 
     def gather(way, c):
-        slot = 1 if way == 0 else 3 - middle.astype(jnp.int32)
+        slot = 1 + way
         return pltpu.make_async_remote_copy(
             src_ref=mod.at[0, c], dst_ref=mod.at[slot, c], send_sem=gs.at[way, c], recv_sem=gr.at[slot, c],
             device_id={"uly": inner if way else near}, device_id_type=MESH)
@@ -86,6 +86,11 @@
         return pltpu.make_async_remote_copy(
             src_ref=mod.at[k, c], dst_ref=mod.at[k, c], send_sem=fs.at[k, c], recv_sem=gr.at[k, c],
             device_id={"uly": near}, device_id_type=MESH)
+
+    def across(c):
+        return pltpu.make_async_remote_copy(
+            src_ref=mod.at[1, c], dst_ref=mod.at[3, c], send_sem=fs.at[1, c], recv_sem=gr.at[3, c],
+            device_id={"uly": inner}, device_id_type=MESH)
 
     @pl.when(middle)
     def _():
@@ -95,9 +100,8 @@
 
     @pl.when(jnp.logical_not(middle))
     def _():
-        for way in (0, 1):
-            for c in range(chunks):
-                gather(way, c).start()
+        for c in range(chunks):
+            gather(0, c).start()
 
     for load in loads[3:6]:
         load.wait()
@@ -212,6 +216,10 @@
             @pl.when((k > 0) & (jnp.logical_not(middle) | (k == 1)))
             def _():
                 landed(k, c).wait_recv()
+
+            @pl.when(middle & (k == 1))
+            def _():
+                across(c).start()
 
             @pl.when(middle & (k > 0) & (k < 3))
             def _():
@@ -439,12 +447,14 @@
         near_to(n).wait_recv()
         settle(n, True)
 
-    for way in (0, 1):
+    for c in range(chunks):
+        gather(0, c).wait_send()
+
+    @pl.when(middle)
+    def _():
         for c in range(chunks):
-            gather(way, c).wait_send()
-
-    @pl.when(middle)
-    def _():
+            gather(1, c).wait_send()
+            across(c).wait_send()
         for k in (2, 3):
             for c in range(chunks):
                 forward(k, c).wait_send()

time: 47.5 us -> 46.3 us (0.975)
  Pallas kernels: 45.7 us -> 44.5 us
    pallas_call x1, Pallas kernels: 45.7 us -> 44.5 us  [fused(): pl.pallas_call(functools.partial(kernel, nb), out_shape=jax.ShapeDtypeStr...]
where the time goes in v5:
time: 46.3 us; the launch traced here: 46.1 us
  Pallas kernels  44.5 us (96%)
  local copies, waits for them, and re-layouts  1.62 us (3%)
    pallas_call x1, Pallas kernels, fused(): pl.pallas_call(functools.partial(kernel, nb), out_shape=jax.ShapeDtypeStr...  44.5 us
    unnamed x1, local copies, waits for them, and re-layouts  1.62 us

profile of v5, /device:TPU:0, one launch (start us, length us, event | category | flops | bytes accessed | tf_op | source)
XLA Modules:
  0.0 46.1 jit_solution(7021870038862446247)
XLA Ops:
  0.0 44.5 %shard_map.91 = bf16[48,2048]{1,0:T(8,128)(2,1)} custom-call(bf16[48,2048]{1,0:T(8,128)(2,1)} %tok_h.1, f32[1,2048]{1,0:T(1,128)} %bitcast.4, f32[1,2048]{1,0:T(1,128)} %bitcast.5, f32[1,2048]{1,0:T(1,128)} %bitcast.6, f32[1,32]{1,0:T(1,128)} %bitcast.7, bf16[2048,512]{1,0:T(8,128)(2,1)} %wq.1, bf16[2048,512]{1,0:T(8,128)(2,1)} %wk.1, bf16[2048,512]{1,0:T(8,128)(2,1)} %wv.1, ...), custom_call_target="tpu_custom_call" | custom-call | tf_op jit(solution)/shard_map/pallas_call | solution.py:505
  44.5 1.6 %copy.11 = bf16[48,2048]{1,0:T(8,128)(2,1)} copy(bf16[48,2048]{1,0:T(8,128)(2,1)} %shard_map.91) | data formatting | bytes 393216

commit v6 on v5

--- a/solution.py
+++ b/solution.py
@@ -18,7 +18,7 @@
 
 def kernel(
     nb, tok_h, shift_h, scale_h, gate_h, gain_h, wq, wk, wv, wo, out,
-    tok, shift, scale, gate, gain, mod, wq_v, wk_v, wv_v, wo_v, kv_s, q_s, kv_r, q_r, vt, top_v, sum_v, acc_v,
+    tok, shift, scale, gate, gain, mod, wq_v, wk_v, wv_v, wo_v, kv_s, q_s, kv_r, q_r, q_v, vt, top_v, sum_v, acc_v,
     att_s, att_r, full_v, full_r, twin_v, part_v, part_s, pair_r, near_r, far_r,
     wsem, gs, gr, fs, hs, hr, bs, br, rs, rr, es, er, ts, tr,
 ):
@@ -106,6 +106,11 @@
     for load in loads[3:6]:
         load.wait()
 
+    most = q_s.shape[2]
+
+    def lower(k, b):
+        return pl.ds(pl.multiple_of((k * nb + b) * most, most), most)
+
     def place(k, b):
         return pl.ds(pl.multiple_of(k * span + b * rows, rows), rows)
 
@@ -115,26 +120,42 @@
     def slab(b):
         return pl.ds(pl.multiple_of(b * depth, depth), depth)
 
-    def twin_out():
-        return pltpu.make_async_remote_copy(
-            src_ref=wo_v.at[slab(mb), apart * tile :], dst_ref=twin_v.at[slab(mb), :], send_sem=ts.at[0, 0],
-            recv_sem=tr.at[mb], device_id={"uly": near}, device_id_type=MESH)
-
-    def twin_in(b):
-        return pltpu.make_async_remote_copy(
-            src_ref=twin_v.at[slab(b), :], dst_ref=twin_v.at[slab(b), :], send_sem=ts.at[0, 0],
-            recv_sem=tr.at[b], device_id={"uly": near}, device_id_type=MESH)
-
-    def twin_share(j):
-        return pltpu.make_async_remote_copy(
-            src_ref=twin_v.at[slab(mb), :], dst_ref=twin_v.at[slab(mb), :], send_sem=ts.at[0, j],
-            recv_sem=tr.at[mb], device_id={"blk": sibling if j == 0 else lax.rem(mb + 2 * j, nb)}, device_id_type=MESH)
-
-    def twin_pass(j):
-        b = lax.rem(mb + 2 * j, nb)
-        return pltpu.make_async_remote_copy(
-            src_ref=twin_v.at[slab(b), :], dst_ref=twin_v.at[slab(b), :], send_sem=ts.at[1, j],
-            recv_sem=tr.at[b], device_id={"blk": sibling}, device_id_type=MESH)
+    half = twin_v.shape[1] // 2
+
+    def twin_copy(p, b, send, who, src=None):
+        here = twin_v.at[slab(b), p * half : (p + 1) * half]
+        return pltpu.make_async_remote_copy(
+            src_ref=here if src is None else src, dst_ref=here, send_sem=send, recv_sem=tr.at[p, b],
+            device_id=who, device_id_type=MESH)
+
+    def twin_out(p):
+        left = apart * tile + p * half
+        return twin_copy(p, mb, ts.at[p, 0, 0], {"uly": near}, wo_v.at[slab(mb), left : left + half])
+
+    def twin_in(p, b):
+        return twin_copy(p, b, ts.at[p, 0, 0], {"uly": near})
+
+    def twin_share(p, j):
+        return twin_copy(p, mb, ts.at[p, 0, j], {"blk": sibling if j == 0 else lax.rem(mb + 2 * j, nb)})
+
+    def twin_pass(p, j):
+        return twin_copy(p, lax.rem(mb + 2 * j, nb), ts.at[p, 1, j], {"blk": sibling})
+
+    def share(p):
+        twin_in(p, mb).wait_recv()
+        for j in range(1, nb // 2):
+            twin_share(p, j).start()
+        twin_share(p, 0).start()
+
+    def relay(p):
+        for j in range(1, nb // 2):
+            twin_in(p, lax.rem(mb + 2 * j, nb)).wait_recv()
+            twin_pass(p, j).start()
+
+    def whole(p):
+        twin_in(p, sibling).wait_recv()
+        for j in range(1, nb // 2):
+            twin_in(p, lax.rem(sibling + 2 * j, nb)).wait_recv()
 
     def full_to(k):
         return pltpu.make_async_remote_copy(
@@ -142,15 +163,15 @@
             device_id={"uly": near}, device_id_type=MESH)
 
     def heads_to(k, kind, b):
-        src, dst = ((kv_s, kv_r), (q_s, q_r))[kind]
-        return pltpu.make_async_remote_copy(
-            src_ref=src.at[k, b], dst_ref=dst.at[place(k, mb), :], send_sem=hs.at[k, kind, b],
+        src, dst, where = ((kv_s, kv_r, place), (q_s, q_r, lower))[kind]
+        return pltpu.make_async_remote_copy(
+            src_ref=src.at[k, b], dst_ref=dst.at[where(k, mb), :], send_sem=hs.at[k, kind, b],
             recv_sem=hr.at[k, kind, mb], device_id={"blk": b}, device_id_type=MESH)
 
     def heads_from(k, kind, b):
-        src, dst = ((kv_s, kv_r), (q_s, q_r))[kind]
-        return pltpu.make_async_remote_copy(
-            src_ref=src.at[k, b], dst_ref=dst.at[place(k, b), :], send_sem=hs.at[k, kind, b],
+        src, dst, where = ((kv_s, kv_r, place), (q_s, q_r, lower))[kind]
+        return pltpu.make_async_remote_copy(
+            src_ref=src.at[k, b], dst_ref=dst.at[where(k, b), :], send_sem=hs.at[k, kind, b],
             recv_sem=hr.at[k, kind, b], device_id={"blk": b}, device_id_type=MESH)
 
     loads[8].wait()
@@ -164,8 +185,17 @@
     def flip(k):
         vt[:, k * span : (k + 1) * span] = kv_r[k * span : (k + 1) * span, :].T[width:, :]
 
+    def widen(k):
+        for b in range(nb):
+            both = q_r[(k * nb + b) * most : (k * nb + b + 1) * most, :]
+            clear = jnp.zeros((most, width), jnp.bfloat16)
+            start = k * span + b * rows
+            q_v[start : start + most, :] = jnp.concatenate([both[:, :width], clear], axis=1)
+            q_v[start + most : start + rows, :] = jnp.concatenate(
+                [both[: rows - most, width:], clear[: rows - most]], axis=1)
+
     def scored(k, c, first, last):
-        q = q_r[k * span + c * SUB : k * span + (c + 1) * SUB, :]
+        q = q_v[k * span + c * SUB : k * span + (c + 1) * SUB, :]
         return lax.dot_general(
             kv_r[first * span : last * span, :], q, (((1,), (1,)), ((), ())), preferred_element_type=jnp.float32)
 
@@ -198,6 +228,7 @@
             await_heads(k, 0)
             await_heads(k, 1)
             flip(k)
+            widen(k)
         for k in (0, 1):
             keep(k, 0, 2)
 
@@ -209,7 +240,8 @@
         @pl.when((k == 1) & jnp.logical_not(middle))
         def _():
             loads[6].wait()
-            twin_out().start()
+            twin_out(0).start()
+            twin_out(1).start()
 
         query = key = value = None
         for c in range(chunks):
@@ -226,14 +258,21 @@
                 landed(k + 1, c).wait_recv()
                 forward(k + 1, c).start()
 
+            if c == 1:
+                @pl.when(middle & (k == 2))
+                def _():
+                    share(0)
+
             x = mod[k, c]
             deeps = slice(c * deep, (c + 1) * deep)
             more_k = jnp.dot(x, wk_v[deeps, :], preferred_element_type=jnp.float32)
             more_v = jnp.dot(x, wv_v[deeps, :], preferred_element_type=jnp.float32)
-            more_q = jnp.dot(x, wq_v[deeps, :], preferred_element_type=jnp.float32)
+            if c < chunks - 1:
+                more_q = jnp.dot(x, wq_v[deeps, :], preferred_element_type=jnp.float32)
             key = more_k if c == 0 else key + more_k
             value = more_v if c == 0 else value + more_v
-            query = more_q if c == 0 else query + more_q
+            if c < chunks - 1:
+                query = more_q if c == 0 else query + more_q
 
         def unit(part):
             power = jnp.mean(part * part, axis=-1, keepdims=True)
@@ -251,12 +290,14 @@
             kv_s[k, h] = jnp.concatenate([unit(key[:, cols]), value[:, cols]], axis=1).astype(jnp.bfloat16)
         send(0)
         kv_r[place(k, mb), :] = kv_s[k, mb]
+        query = query + jnp.dot(x, wq_v[deeps, :], preferred_element_type=jnp.float32)
         for h in range(nb):
             cols = slice(h * width, (h + 1) * width)
             line = unit(query[:, cols])
-            q_s[k, h] = jnp.concatenate([line, jnp.zeros_like(line)], axis=1).astype(jnp.bfloat16)
+            rest = jnp.concatenate([line[most:], jnp.zeros((2 * most - rows, width), jnp.float32)], axis=0)
+            q_s[k, h] = jnp.concatenate([line[:most], rest], axis=1).astype(jnp.bfloat16)
         send(1)
-        q_r[place(k, mb), :] = q_s[k, mb]
+        q_r[lower(k, mb), :] = q_s[k, mb]
         return carry
 
     lax.fori_loop(0, 4, piece, 0)
@@ -264,16 +305,18 @@
     @pl.when(middle)
     def _():
         loads[6].wait()
-        twin_in(mb).wait_recv()
-        for j in range(1, nb // 2):
-            twin_share(j).start()
-        twin_share(0).start()
+        share(1)
         first_attend()
 
     await_heads(2, 0)
     await_heads(2, 1)
     flip(2)
+    widen(2)
     keep(2, 0, 3)
+    @pl.when(middle)
+    def _():
+        relay(0)
+
     await_heads(3, 0)
     flip(3)
 
@@ -298,6 +341,7 @@
         if j == 0:
             lower = [finished(2, c) for c in range(span // SUB)]
             await_heads(3, 1)
+            widen(3)
             upper = [finished(3, c) for c in range(span // SUB)]
         else:
             lower = [finished(1, c) for c in range(span // SUB)]
@@ -393,9 +437,7 @@
 
     @pl.when(middle)
     def _():
-        for j in range(1, nb // 2):
-            twin_in(lax.rem(mb + 2 * j, nb)).wait_recv()
-            twin_pass(j).start()
+        relay(1)
 
     loads[7].wait()
     project(0)
@@ -407,12 +449,14 @@
 
     @pl.when(middle)
     def _():
-        twin_in(sibling).wait_recv()
-        for j in range(1, nb // 2):
-            twin_in(lax.rem(sibling + 2 * j, nb)).wait_recv()
         for k in (3, 2):
             full_to(k).wait_recv()
             for n in range(apart, parts):
+                if k == 3:
+                    if n == apart:
+                        whole(0)
+                    if n == (apart + parts) // 2:
+                        whole(1)
                 part_s[k, n] = (part_v[k, n] + twin(k, n)).astype(jnp.bfloat16)
                 far_to(k, n).start()
             for n in range(apart):
@@ -479,14 +523,16 @@
         for k in (1, 2, 3):
             for n in range(apart, parts):
                 near_to(n).wait_send() if k == 1 else pair_to(k, n).wait_send()
-        for j in range(nb // 2):
-            twin_share(j).wait_send()
-        for j in range(1, nb // 2):
-            twin_pass(j).wait_send()
+        for p in (0, 1):
+            for j in range(nb // 2):
+                twin_share(p, j).wait_send()
+            for j in range(1, nb // 2):
+                twin_pass(p, j).wait_send()
 
     @pl.when(jnp.logical_not(middle))
     def _():
-        twin_out().wait_send()
+        twin_out(0).wait_send()
+        twin_out(1).wait_send()
         for k in (1, 2, 3):
             full_to(k).wait_send()
 
@@ -498,6 +544,7 @@
     tile = 512
     parts = D // tile
     span = nb * rows
+    most = -(-rows // 32) * 16
     bf16, f32 = jnp.bfloat16, jnp.float32
     vmem = pl.BlockSpec(memory_space=pltpu.VMEM)
     hbm = pl.BlockSpec(memory_space=pltpu.HBM)
@@ -519,8 +566,9 @@
             pltpu.VMEM((D, cols), bf16),
             pltpu.VMEM((cols, D), bf16),
             pltpu.VMEM((4, nb, rows, 128), bf16),
-            pltpu.VMEM((4, nb, rows, 128), bf16),
+            pltpu.VMEM((4, nb, most, 128), bf16),
             pltpu.VMEM((4 * span, 128), bf16),
+            pltpu.VMEM((4 * nb * most, 128), bf16),
             pltpu.VMEM((4 * span, 128), bf16),
             pltpu.VMEM((64, 4 * span), bf16),
             pltpu.VMEM((4, 1, span), f32),
@@ -548,8 +596,8 @@
             dma((4, parts)),
             dma((4,)),
             dma((4,)),
-            dma((2, nb // 2)),
-            dma((nb,)),
+            dma((2, 2, nb // 2)),
+            dma((2, nb)),
         ],
         compiler_params=pltpu.CompilerParams(
             collective_id=0, has_side_effects=True, vmem_limit_bytes=56 * 1024 * 1024

time: 46.3 us -> 45.6 us (0.985)
  Pallas kernels: 44.5 us -> 43.8 us
    pallas_call x1, Pallas kernels: 44.5 us -> 43.8 us  [fused(): pl.pallas_call(functools.partial(kernel, nb), out_shape=jax.ShapeDtypeStr...]
where the time goes in v6:
time: 45.6 us; the launch traced here: 45.4 us
  Pallas kernels  43.8 us (96%)
  local copies, waits for them, and re-layouts  1.62 us (4%)
    pallas_call x1, Pallas kernels, fused(): pl.pallas_call(functools.partial(kernel, nb), out_shape=jax.ShapeDtypeStr...  43.8 us
    unnamed x1, local copies, waits for them, and re-layouts  1.62 us

profile of v6, /device:TPU:0, one launch (start us, length us, event | category | flops | bytes accessed | tf_op | source)
XLA Modules:
  0.0 45.4 jit_solution(13501376889612987950)
XLA Ops:
  0.0 43.8 %shard_map.91 = bf16[48,2048]{1,0:T(8,128)(2,1)} custom-call(bf16[48,2048]{1,0:T(8,128)(2,1)} %tok_h.1, f32[1,2048]{1,0:T(1,128)} %bitcast.4, f32[1,2048]{1,0:T(1,128)} %bitcast.5, f32[1,2048]{1,0:T(1,128)} %bitcast.6, f32[1,32]{1,0:T(1,128)} %bitcast.7, bf16[2048,512]{1,0:T(8,128)(2,1)} %wq.1, bf16[2048,512]{1,0:T(8,128)(2,1)} %wk.1, bf16[2048,512]{1,0:T(8,128)(2,1)} %wv.1, ...), custom_call_target="tpu_custom_call" | custom-call | tf_op jit(solution)/shard_map/pallas_call | solution.py:552
  43.8 1.6 %copy.11 = bf16[48,2048]{1,0:T(8,128)(2,1)} copy(bf16[48,2048]{1,0:T(8,128)(2,1)} %shard_map.91) | data formatting | bytes 393216

commit v7 on v6

--- a/solution.py
+++ b/solution.py
@@ -265,14 +265,13 @@
 
             x = mod[k, c]
             deeps = slice(c * deep, (c + 1) * deep)
-            more_k = jnp.dot(x, wk_v[deeps, :], preferred_element_type=jnp.float32)
-            more_v = jnp.dot(x, wv_v[deeps, :], preferred_element_type=jnp.float32)
+            more_q = jnp.dot(x, wq_v[deeps, :], preferred_element_type=jnp.float32)
+            query = more_q if c == 0 else query + more_q
             if c < chunks - 1:
-                more_q = jnp.dot(x, wq_v[deeps, :], preferred_element_type=jnp.float32)
-            key = more_k if c == 0 else key + more_k
-            value = more_v if c == 0 else value + more_v
-            if c < chunks - 1:
-                query = more_q if c == 0 else query + more_q
+                more_k = jnp.dot(x, wk_v[deeps, :], preferred_element_type=jnp.float32)
+                more_v = jnp.dot(x, wv_v[deeps, :], preferred_element_type=jnp.float32)
+                key = more_k if c == 0 else key + more_k
+                value = more_v if c == 0 else value + more_v
 
         def unit(part):
             power = jnp.mean(part * part, axis=-1, keepdims=True)
@@ -285,12 +284,6 @@
 
             lax.fori_loop(1, nb, one, 0)
 
-        for h in range(nb):
-            cols = slice(h * width, (h + 1) * width)
-            kv_s[k, h] = jnp.concatenate([unit(key[:, cols]), value[:, cols]], axis=1).astype(jnp.bfloat16)
-        send(0)
-        kv_r[place(k, mb), :] = kv_s[k, mb]
-        query = query + jnp.dot(x, wq_v[deeps, :], preferred_element_type=jnp.float32)
         for h in range(nb):
             cols = slice(h * width, (h + 1) * width)
             line = unit(query[:, cols])
@@ -298,6 +291,13 @@
             q_s[k, h] = jnp.concatenate([line[:most], rest], axis=1).astype(jnp.bfloat16)
         send(1)
         q_r[lower(k, mb), :] = q_s[k, mb]
+        key = key + jnp.dot(x, wk_v[deeps, :], preferred_element_type=jnp.float32)
+        value = value + jnp.dot(x, wv_v[deeps, :], preferred_element_type=jnp.float32)
+        for h in range(nb):
+            cols = slice(h * width, (h + 1) * width)
+            kv_s[k, h] = jnp.concatenate([unit(key[:, cols]), value[:, cols]], axis=1).astype(jnp.bfloat16)
+        send(0)
+        kv_r[place(k, mb), :] = kv_s[k, mb]
         return carry
 
     lax.fori_loop(0, 4, piece, 0)
@@ -317,6 +317,9 @@
     def _():
         relay(0)
 
+    await_heads(3, 1)
+    widen(3)
+    keep(3, 0, 3)
     await_heads(3, 0)
     flip(3)
 
@@ -331,17 +334,12 @@
             send_sem=bs.at[j, b], recv_sem=br.at[j, b], device_id={"blk": b}, device_id_type=MESH)
 
     def finished(k, c):
-        if k == 3:
-            unused, total, summed = begin(k, c, 0, 4)
-        else:
-            total, summed = more(k, c, 3 if k == 2 else 2, 4)
+        total, summed = more(k, c, 3 if k > 1 else 2, 4)
         return summed / total
 
     def finish(j):
         if j == 0:
             lower = [finished(2, c) for c in range(span // SUB)]
-            await_heads(3, 1)
-            widen(3)
             upper = [finished(3, c) for c in range(span // SUB)]
         else:
             lower = [finished(1, c) for c in range(span // SUB)]
@@ -551,7 +549,7 @@
     dma = pltpu.SemaphoreType.DMA
     return pl.pallas_call(
         functools.partial(kernel, nb),
-        out_shape=jax.ShapeDtypeStruct((rows, D), bf16),
+        out_shape=pltpu.VMEM((rows, D), bf16),
         in_specs=[hbm] * 9,
         out_specs=vmem,
         scratch_shapes=[

time: 45.6 us -> 44.2 us (0.969); the launches traced: 45.4 us -> 43.3 us
  Pallas kernels: 43.8 us -> 42.6 us
  local copies, waits for them, and re-layouts: 1.62 us -> 0.68 us
    pallas_call x1, Pallas kernels: 43.8 us -> 42.6 us  [fused(): pl.pallas_call(functools.partial(kernel, nb), out_shape=pltpu.VMEM((rows,...]
    unnamed x1, local copies, waits for them, and re-layouts: 1.62 us -> 0.68 us
where the time goes in v7:
time: 44.2 us; the launch traced here: 43.3 us
  Pallas kernels  42.6 us (96%)
  local copies, waits for them, and re-layouts  0.68 us (2%)
    pallas_call x1, Pallas kernels, fused(): pl.pallas_call(functools.partial(kernel, nb), out_shape=pltpu.VMEM((rows,...  42.6 us

profile of v7, /device:TPU:0, one launch (start us, length us, event | category | flops | bytes accessed | tf_op | source)
XLA Modules:
  0.0 43.3 jit_solution(11301985980484469856)
XLA Ops:
  0.0 42.6 %shard_map.91 = bf16[48,2048]{1,0:T(8,128)(2,1)S(1)} custom-call(bf16[48,2048]{1,0:T(8,128)(2,1)} %tok_h.1, f32[1,2048]{1,0:T(1,128)} %bitcast.4, f32[1,2048]{1,0:T(1,128)} %bitcast.5, f32[1,2048]{1,0:T(1,128)} %bitcast.6, f32[1,32]{1,0:T(1,128)} %bitcast.7, bf16[2048,512]{1,0:T(8,128)(2,1)} %wq.1, bf16[2048,512]{1,0:T(8,128)(2,1)} %wk.1, ...), custom_call_target="tpu_custom_call" | custom-call | tf_op jit(solution)/shard_map/pallas_call | solution.py:550
  42.6 0.7 %copy.11 = bf16[48,2048]{1,0:T(8,128)(2,1)} copy(bf16[48,2048]{1,0:T(8,128)(2,1)S(1)} %shard_map.91) | data formatting | bytes 393216

commit v8 on v6

--- a/solution.py
+++ b/solution.py
@@ -20,7 +20,7 @@
     nb, tok_h, shift_h, scale_h, gate_h, gain_h, wq, wk, wv, wo, out,
     tok, shift, scale, gate, gain, mod, wq_v, wk_v, wv_v, wo_v, kv_s, q_s, kv_r, q_r, q_v, vt, top_v, sum_v, acc_v,
     att_s, att_r, full_v, full_r, twin_v, part_v, part_s, pair_r, near_r, far_r,
-    wsem, gs, gr, fs, hs, hr, bs, br, rs, rr, es, er, ts, tr,
+    wsem, gs, gr, fs, hs, hr, bs, br, rs, rr, es, er, ts, tr, ready,
 ):
     width = D // HEADS
     rows = tok.shape[0]
@@ -38,15 +38,19 @@
     outer = 3 - 3 * high
 
     barrier = pltpu.get_barrier_semaphore()
-    for z in (inner, near):
-        pl.semaphore_signal(barrier, inc=1, device_id={"uly": z}, device_id_type=MESH)
+    core = lax.rem(mb, 2)
+    beside = mb + 2 - 4 * lax.rem(mb // 2, 2)
+    behind = mb + 4 - 8 * (mb // 4)
+    pl.semaphore_signal(barrier, inc=1, device_id={"uly": near}, device_id_type=MESH)
 
     @pl.when(middle)
     def _():
-        pl.semaphore_signal(barrier, inc=1, device_id={"uly": outer}, device_id_type=MESH)
-
-    for j in range(1, nb):
-        pl.semaphore_signal(barrier, inc=1, device_id={"blk": lax.rem(mb + j, nb)}, device_id_type=MESH)
+        pl.semaphore_signal(barrier, inc=1, device_id={"uly": inner}, device_id_type=MESH)
+
+    for b in (mb, beside, behind):
+        if b is not mb:
+            pl.semaphore_signal(barrier, inc=1, device_id={"blk": b}, device_id_type=MESH)
+        pl.semaphore_signal(barrier, inc=1, device_id={"blk": b + 1 - 2 * core}, device_id_type=MESH)
 
     pairs = (
         (tok_h, tok), (shift_h, shift), (scale_h, scale), (wk, wk_v), (wv, wv_v), (wq, wq_v),
@@ -69,7 +73,8 @@
     for c in range(chunks):
         mod[0, c] = modded[:, c * deep : (c + 1) * deep]
 
-    pl.semaphore_wait(barrier, nb + 1 + middle.astype(jnp.int32))
+    pl.semaphore_wait(barrier, 6 + middle.astype(jnp.int32))
+    pl.semaphore_signal(ready, inc=1, device_id={"blk": beside}, device_id_type=MESH)
 
     def gather(way, c):
         slot = 1 + way
@@ -105,6 +110,7 @@
 
     for load in loads[3:6]:
         load.wait()
+    pl.semaphore_wait(ready, 1)
 
     most = q_s.shape[2]
 
@@ -551,7 +557,7 @@
     dma = pltpu.SemaphoreType.DMA
     return pl.pallas_call(
         functools.partial(kernel, nb),
-        out_shape=jax.ShapeDtypeStruct((rows, D), bf16),
+        out_shape=pltpu.VMEM((rows, D), bf16),
         in_specs=[hbm] * 9,
         out_specs=vmem,
         scratch_shapes=[
@@ -598,6 +604,7 @@
             dma((4,)),
             dma((2, 2, nb // 2)),
             dma((2, nb)),
+            pltpu.SemaphoreType.REGULAR,
         ],
         compiler_params=pltpu.CompilerParams(
             collective_id=0, has_side_effects=True, vmem_limit_bytes=56 * 1024 * 1024
@@ -709,6 +716,6 @@
     out_specs = P(("blk", "uly"), None)
     nb, nz = mesh.shape["blk"], mesh.shape["uly"]
     run = body
-    if HEADS == nb * nz and nz == 4 and nb % 2 == 0:
+    if HEADS == nb * nz and nz == 4 and nb == 8:
         run = functools.partial(fused, nb)
     return jax.shard_map(run, mesh=mesh, in_specs=in_specs, out_specs=out_specs, check_vma=False)

time: 45.6 us -> 44 us (0.965); the launches traced: 45.4 us -> 43.1 us
  Pallas kernels: 43.8 us -> 42.4 us
  local copies, waits for them, and re-layouts: 1.62 us -> 0.68 us
    pallas_call x1, Pallas kernels: 43.8 us -> 42.4 us  [fused(): pl.pallas_call(functools.partial(kernel, nb), out_shape=pltpu.VMEM((rows,...]
    unnamed x1, local copies, waits for them, and re-layouts: 1.62 us -> 0.68 us
where the time goes in v8:
time: 44 us; the launch traced here: 43.1 us
  Pallas kernels  42.4 us (96%)
  local copies, waits for them, and re-layouts  0.68 us (2%)
    pallas_call x1, Pallas kernels, fused(): pl.pallas_call(functools.partial(kernel, nb), out_shape=pltpu.VMEM((rows,...  42.4 us

profile of v8, /device:TPU:0, one launch (start us, length us, event | category | flops | bytes accessed | tf_op | source)
XLA Modules:
  0.0 43.1 jit_solution(3632371787476182702)
XLA Ops:
  0.0 42.4 %shard_map.91 = bf16[48,2048]{1,0:T(8,128)(2,1)S(1)} custom-call(bf16[48,2048]{1,0:T(8,128)(2,1)} %tok_h.1, f32[1,2048]{1,0:T(1,128)} %bitcast.4, f32[1,2048]{1,0:T(1,128)} %bitcast.5, f32[1,2048]{1,0:T(1,128)} %bitcast.6, f32[1,32]{1,0:T(1,128)} %bitcast.7, bf16[2048,512]{1,0:T(8,128)(2,1)} %wq.1, bf16[2048,512]{1,0:T(8,128)(2,1)} %wk.1, ...), custom_call_target="tpu_custom_call" | custom-call | tf_op jit(solution)/shard_map/pallas_call | solution.py:558
  42.4 0.7 %copy.11 = bf16[48,2048]{1,0:T(8,128)(2,1)} copy(bf16[48,2048]{1,0:T(8,128)(2,1)S(1)} %shard_map.91) | data formatting | bytes 393216

commit v9 on v8

--- a/solution.py
+++ b/solution.py
@@ -37,21 +37,6 @@
     inner = 2 - high
     outer = 3 - 3 * high
 
-    barrier = pltpu.get_barrier_semaphore()
-    core = lax.rem(mb, 2)
-    beside = mb + 2 - 4 * lax.rem(mb // 2, 2)
-    behind = mb + 4 - 8 * (mb // 4)
-    pl.semaphore_signal(barrier, inc=1, device_id={"uly": near}, device_id_type=MESH)
-
-    @pl.when(middle)
-    def _():
-        pl.semaphore_signal(barrier, inc=1, device_id={"uly": inner}, device_id_type=MESH)
-
-    for b in (mb, beside, behind):
-        if b is not mb:
-            pl.semaphore_signal(barrier, inc=1, device_id={"blk": b}, device_id_type=MESH)
-        pl.semaphore_signal(barrier, inc=1, device_id={"blk": b + 1 - 2 * core}, device_id_type=MESH)
-
     pairs = (
         (tok_h, tok), (shift_h, shift), (scale_h, scale), (wk, wk_v), (wv, wv_v), (wq, wq_v),
         (wo, wo_v), (gate_h, gate), (gain_h, gain),
@@ -60,7 +45,25 @@
         pltpu.make_async_copy(src, dst, wsem.at[i])
         for i, (src, dst) in enumerate(pairs)
     ]
-    for load in loads:
+    for load in loads[:3]:
+        load.start()
+
+    barrier = pltpu.get_barrier_semaphore()
+    core = lax.rem(mb, 2)
+    beside = mb + 2 - 4 * lax.rem(mb // 2, 2)
+    behind = mb + 4 - 8 * (mb // 4)
+    pl.semaphore_signal(barrier, inc=1, device_id={"uly": near}, device_id_type=MESH)
+
+    @pl.when(middle)
+    def _():
+        pl.semaphore_signal(barrier, inc=1, device_id={"uly": inner}, device_id_type=MESH)
+
+    for b in (mb, beside, behind):
+        if b is not mb:
+            pl.semaphore_signal(barrier, inc=1, device_id={"blk": b}, device_id_type=MESH)
+        pl.semaphore_signal(barrier, inc=1, device_id={"blk": b + 1 - 2 * core}, device_id_type=MESH)
+
+    for load in loads[3:]:
         load.start()
     for load in loads[:3]:
         load.wait()
@@ -239,10 +242,6 @@
             keep(k, 0, 2)
 
     def piece(k, carry):
-        @pl.when((k == 3) & jnp.logical_not(middle))
-        def _():
-            first_attend()
-
         @pl.when((k == 1) & jnp.logical_not(middle))
         def _():
             loads[6].wait()
@@ -312,8 +311,8 @@
     def _():
         loads[6].wait()
         share(1)
-        first_attend()
-
+
+    first_attend()
     await_heads(2, 0)
     await_heads(2, 1)
     flip(2)

time: 44 us -> 43.7 us (level)
  no operation moved by 1% of the time
where the time goes in v9:
time: 43.7 us; the launch traced here: 43.1 us
  Pallas kernels  42.4 us (97%)
  local copies, waits for them, and re-layouts  0.68 us (2%)
    pallas_call x1, Pallas kernels, fused(): pl.pallas_call(functools.partial(kernel, nb), out_shape=pltpu.VMEM((rows,...  42.4 us

profile of v9, /device:TPU:0, one launch (start us, length us, event | category | flops | bytes accessed | tf_op | source)
XLA Modules:
  0.0 43.1 jit_solution(7251830820276114740)
XLA Ops:
  0.0 42.4 %shard_map.91 = bf16[48,2048]{1,0:T(8,128)(2,1)S(1)} custom-call(bf16[48,2048]{1,0:T(8,128)(2,1)} %tok_h.1, f32[1,2048]{1,0:T(1,128)} %bitcast.4, f32[1,2048]{1,0:T(1,128)} %bitcast.5, f32[1,2048]{1,0:T(1,128)} %bitcast.6, f32[1,32]{1,0:T(1,128)} %bitcast.7, bf16[2048,512]{1,0:T(8,128)(2,1)} %wq.1, bf16[2048,512]{1,0:T(8,128)(2,1)} %wk.1, ...), custom_call_target="tpu_custom_call" | custom-call | tf_op jit(solution)/shard_map/pallas_call | solution.py:557
  42.4 0.7 %copy.11 = bf16[48,2048]{1,0:T(8,128)(2,1)} copy(bf16[48,2048]{1,0:T(8,128)(2,1)S(1)} %shard_map.91) | data formatting | bytes 393216
